TPU v7x, 128 devices: a whole 4x4x4 slice. The times are simulated.
128 devices in a mesh: member: 32 (over z, x, core), section: 4 (over y).
Axes of the slice: x: 4, y: 4, z: 4, core: 2. Of those that a mesh axis runs over, the one named last changes fastest.
Arguments:
- inputs: bfloat16 [32, 2, 1, 14, 14, 512], P('member'), may hold values from -6 to 6
- cotangent: bfloat16 [32, 2, 1, 14, 14, 512], P('member'), may hold values from -6 to 6
- probe: bfloat16 [32, 1, 14, 14, 512], P('member'), may hold values from -6 to 6
- dw_kernel: float32 [32, 4, 7, 7, 512], P('member', 'section'), may hold values from -0.875 to 0.875
- dw_bias: float32 [32, 4, 512], P('member', 'section'), may hold values from -3 to 3
- norm_gain: float32 [32, 4, 512], P('member', 'section'), may hold values from 0.5 to 1.5
- norm_bias: float32 [32, 4, 512], P('member', 'section'), may hold values from -3 to 3
- w_in: float32 [32, 4, 512, 2048], P('member', 'section'), may hold values from -0.25 to 0.25
- b_in: float32 [32, 4, 2048], P('member', 'section'), may hold values from -3 to 3
- w_out: float32 [32, 4, 2048, 512], P('member', 'section'), may hold values from -0.125 to 0.125
- b_out: float32 [32, 4, 512], P('member', 'section'), may hold values from -3 to 3
- layer_scale: float32 [32, 4, 512], P('member', 'section'), may hold values from 0.3 to 1.5
- shuffle_mask: int32 [4, 32], P('section'), may hold values from 0 to 1, as said below
- source_member: int32 [4, 32, 32], P('section'), may hold values from 0 to 31, as said below
Outputs:
- new_w_in: float32 [32, 4, 512, 2048], P('member', 'section')
- new_w_out: float32 [32, 4, 2048, 512], P('member', 'section')
- features: bfloat16 [32, 4, 1, 14, 14, 512], P('member', 'section')
Inputs may be any that keep to these rules, and one draw needn't show every extreme that they name: `shuffle_mask`: each section marks exactly 16 of its 32 blocks. Each source_member[s, k] is a permutation of the members. For the marked blocks of a section no member is its own source, and no member is the source of more than 1 of another member's blocks; some pair of members reaches 1 in every section.
All inputs are finite; a program needn't handle non-finite values.
Results may differ from a plain program's by a relative error of at most 0.014.
Values may be sent and summed in bfloat16 or wider, within the bound.
A program may use at most 192 MiB of HBM per device.

v0:
```python
import jax
import jax.numpy as jnp
from jax import lax
from jax.sharding import PartitionSpec as P

TILE = 128


learning_rate = 0.001
norm_epsilon = 1e-06


def from_behind(value, axis, steps):
    count = lax.axis_size(axis)
    first, last = (max(0, -steps), min(count, count - steps))
    return lax.ppermute(value, axis, [(source, source + steps) for source in range(first, last)])


def depthwise(widened, kernel):
    height = widened.shape[1]
    width = widened.shape[2]
    padded = jnp.pad(widened, ((0, 0), (3, 3), (3, 3), (0, 0)))
    total = jnp.zeros(widened.shape, jnp.float32)
    for row_off in range(7):
        for col_off in range(7):
            total = (
                total
                + kernel[row_off, col_off]
                * padded[:, row_off : row_off + height, col_off : col_off + width, :]
            )
    return total


def block(params, incoming):
    (
        kernel,
        conv_bias,
        gain,
        shift_bias,
        first_weight,
        first_bias,
        second_weight,
        second_bias,
        scale,
    ) = params
    widened = incoming.astype(jnp.float32)
    channels = widened.shape[-1]
    spread = depthwise(widened, kernel) + conv_bias
    center = jnp.mean(spread, axis=-1, keepdims=True)
    offset = spread - center
    variance = jnp.mean(offset * offset, axis=-1, keepdims=True)
    normed = (offset * lax.rsqrt(variance + norm_epsilon) * gain + shift_bias).astype(jnp.bfloat16)
    rows = normed.reshape(-1, channels)
    hidden = jax.nn.gelu(
        jnp.dot(rows, first_weight, preferred_element_type=jnp.float32) + first_bias,
        approximate=False,
    ).astype(jnp.bfloat16)
    mixed = jnp.dot(hidden, second_weight, preferred_element_type=jnp.float32) + second_bias
    return (widened + scale * mixed.reshape(widened.shape)).astype(jnp.bfloat16)


def lowered(params):
    return tuple(
        (
            leaf.astype(jnp.bfloat16) if position in (4, 6) else leaf
            for position, leaf in enumerate(params)
        )
    )


def pass_on(values):
    return from_behind(values, "section", 1)


def shuffle(first, second, marked, sources):
    member = lax.axis_index("member")
    members = lax.axis_size("member")
    blocks = marked.shape[0]
    capacity = (blocks // 2 + members - 2) // (members - 1)
    slots = members * capacity
    channels = first.shape[0]
    tile_count = first.shape[1] // TILE
    row_groups = second.shape[0] // channels
    column_tiles = channels // TILE
    member_ids = jnp.arange(members, dtype=jnp.int32)
    target = jnp.sum(jnp.where(sources == member, member_ids[None, :], 0), axis=1)
    anchor = lax.dynamic_index_in_dim(sources, member, axis=1, keepdims=False)
    block_ids = jnp.arange(blocks, dtype=jnp.int32)
    earlier = block_ids[:, None] > block_ids[None, :]
    counted = marked[None, :] == 1
    out_rank = jnp.sum(earlier & (target[:, None] == target[None, :]) & counted, axis=1)
    in_rank = jnp.sum(earlier & (anchor[:, None] == anchor[None, :]) & counted, axis=1)
    out_slot = target * capacity + out_rank
    in_slot = jnp.clip(anchor * capacity + in_rank, 0, slots - 1)
    slot_ids = jnp.arange(slots, dtype=jnp.int32)
    matches = (slot_ids[:, None] == out_slot[None, :]) & counted
    slot_used = jnp.any(matches, axis=1)
    slot_block = jnp.sum(jnp.where(matches, block_ids[None, :], 0), axis=1)
    first_tiles = jnp.transpose(first.reshape(channels, tile_count, TILE), (1, 0, 2))
    second_tiles = jnp.transpose(
        second.reshape(row_groups, channels, column_tiles, TILE), (2, 0, 1, 3)
    ).reshape(column_tiles * row_groups, channels, TILE)
    all_tiles = jnp.concatenate([first_tiles, second_tiles], axis=0)
    outgoing = jnp.where(slot_used[:, None, None], jnp.take(all_tiles, slot_block, axis=0), 0.0)
    incoming = lax.all_to_all(
        outgoing.astype(jnp.bfloat16), "member", split_axis=0, concat_axis=0, tiled=True
    ).astype(outgoing.dtype)
    new_tiles = jnp.where(
        (marked == 1)[:, None, None], jnp.take(incoming, in_slot, axis=0), all_tiles
    )
    new_first = jnp.transpose(new_tiles[:tile_count], (1, 0, 2)).reshape(first.shape)
    new_second = jnp.transpose(
        new_tiles[tile_count:].reshape(column_tiles, row_groups, channels, TILE), (1, 2, 0, 3)
    ).reshape(second.shape)
    return (new_first, new_second)


def local(
    inputs,
    cotangent,
    probe,
    dw_kernel,
    dw_bias,
    norm_gain,
    norm_bias,
    w_in,
    b_in,
    w_out,
    b_out,
    layer_scale,
    shuffle_mask,
    source_member,
):
    sections = lax.axis_size("section")
    section = lax.axis_index("section")
    micro_count = inputs.shape[1]
    floats = (
        dw_kernel[0, 0],
        dw_bias[0, 0],
        norm_gain[0, 0],
        norm_bias[0, 0],
        w_in[0, 0],
        b_in[0, 0],
        w_out[0, 0],
        b_out[0, 0],
        layer_scale[0, 0],
    )
    current_params = lowered(floats)
    images = inputs[0]
    slopes = cotangent[0]
    empty = jnp.zeros(images.shape[1:], jnp.bfloat16)
    stored = [empty for position in range(micro_count)]
    received = empty
    ticks = micro_count + sections - 1
    for tick in range(ticks):
        entry = images[min(tick, micro_count - 1)]
        current = jnp.where(section == 0, entry, received)
        which = tick - section
        stored = [
            jnp.where(which == position, current, kept) for position, kept in enumerate(stored)
        ]
        if tick < ticks - 1:
            received = pass_on(block(current_params, current))
    totals = tuple((jnp.zeros(leaf.shape, jnp.float32) for leaf in current_params))
    returning = empty
    for tick in range(ticks):
        which = tick - (sections - 1 - section)
        active = (which >= 0) & (which < micro_count)
        source = stored[0]
        slope = slopes[0]
        position = 1
        source = jnp.where(which == position, stored[position], source)
        slope = jnp.where(which == position, slopes[position], slope)
        slope = jnp.where(section == sections - 1, slope, returning)
        unused, pull = jax.vjp(block, current_params, source)
        delta, back = pull(slope)
        totals = tuple(
            (
                total + jnp.where(active, piece.astype(jnp.float32), 0.0)
                for total, piece in zip(totals, delta)
            )
        )
        if tick < ticks - 1:
            returning = from_behind(back, "section", -1)
    updated = tuple((leaf - learning_rate * total for leaf, total in zip(floats, totals)))
    new_first, new_second = shuffle(updated[4], updated[6], shuffle_mask[0], source_member[0])
    final_params = lowered(
        (
            updated[0],
            updated[1],
            updated[2],
            updated[3],
            new_first,
            updated[5],
            new_second,
            updated[7],
            updated[8],
        )
    )
    received = jnp.zeros(probe.shape[1:], jnp.bfloat16)
    kept_out = received
    for tick in range(sections):
        current = jnp.where(section == 0, probe[0], received)
        result = block(final_params, current)
        kept_out = jnp.where(section == tick, result, kept_out)
        if tick < sections - 1:
            received = pass_on(result)
    return (new_first[None, None], new_second[None, None], kept_out[None, None])


def solution(mesh):
    return jax.shard_map(
        local,
        mesh=mesh,
        in_specs=(
            P("member", None, None, None, None, None),
            P("member", None, None, None, None, None),
            P("member", None, None, None, None),
            P("member", "section", None, None, None),
            P("member", "section", None),
            P("member", "section", None),
            P("member", "section", None),
            P("member", "section", None, None),
            P("member", "section", None),
            P("member", "section", None, None),
            P("member", "section", None),
            P("member", "section", None),
            P("section", None),
            P("section", None, None),
        ),
        out_specs=(
            P("member", "section", None, None),
            P("member", "section", None, None),
            P("member", "section", None, None, None, None),
        ),
        check_vma=False,
    )
```

profile of v0, /device:TPU:8, one launch (start us, length us, event | category | flops | bytes accessed | tf_op | source)
XLA Modules:
  0.0 596.7 jit_solution(3344879547598543498)
XLA Ops:
  9.1 5.6 bitcast_convert_fusion.1
  17.1 7.4 %convolution_add_fusion.21 = f32[196,512]{1,0:T(8,128)} fusion(bf16[2048,512]{1,0:T(8,128)(2,1)} %get-tuple-element.345, bf16[196,512]{1,0:T(8,128)(2,1)S(1)} %reshape.3115, bf16[1,1,512,2048]{3,2,1,0:T(8,128)(2,1)} %get-tuple-element.343, f32[2048]{0:T(1024)S(1)} %bitcast.1700, f32[512]{0:T(512)S(1)} %bitcast.1770), kind=kOutput, calls=%fused_computation.947 | convolution fusion | flops 848676864 | bytes 4806656 | tf_op jit(solution)/shard_map/dot_general | solution.py:58
  39.0 4.6 fusion.1528
  44.8 7.4 %convolution_add_fusion.20 = f32[196,512]{1,0:T(8,128)} fusion(bf16[2048,512]{1,0:T(8,128)(2,1)} %get-tuple-element.345, bf16[196,512]{1,0:T(8,128)(2,1)S(1)} %reshape.3117, bf16[1,1,512,2048]{3,2,1,0:T(8,128)(2,1)} %get-tuple-element.343, f32[2048]{0:T(1024)S(1)} %bitcast.1701, f32[512]{0:T(512)S(1)} %bitcast.1771), kind=kOutput, calls=%fused_computation.946 | convolution fusion | flops 848676864 | bytes 4806656 | tf_op jit(solution)/shard_map/dot_general | solution.py:58
  57.9 4.6 collective-permute-done.1
  67.2 7.3 %convolution_add_fusion.19 = f32[196,512]{1,0:T(8,128)} fusion(bf16[2048,512]{1,0:T(8,128)(2,1)} %get-tuple-element.345, bf16[196,512]{1,0:T(8,128)(2,1)S(1)} %reshape.3119, bf16[1,1,512,2048]{3,2,1,0:T(8,128)(2,1)} %get-tuple-element.343, f32[2048]{0:T(1024)S(1)} %bitcast.1702, f32[512]{0:T(512)S(1)} %bitcast.1772), kind=kOutput, calls=%fused_computation.945 | convolution fusion | flops 848676864 | bytes 4806656 | tf_op jit(solution)/shard_map/dot_general | solution.py:58
  91.2 7.3 %convolution_add_fusion.18 = f32[196,512]{1,0:T(8,128)} fusion(bf16[2048,512]{1,0:T(8,128)(2,1)} %get-tuple-element.345, bf16[196,512]{1,0:T(8,128)(2,1)} %reshape.3121, bf16[1,1,512,2048]{3,2,1,0:T(8,128)(2,1)} %get-tuple-element.343, f32[2048]{0:T(1024)} %bitcast.1694, f32[512]{0:T(512)} %bitcast.1769), kind=kOutput, calls=%fused_computation.944 | convolution fusion | flops 848676864 | bytes 4806656 | tf_op jit(solution)/shard_map/dot_general | solution.py:58
  115.5 3.8 fusion.1517
  123.8 3.8 fusion.1519
  127.9 4.3 fusion.1511
  135.7 6.5 %multiply_convert_fusion.4 = (bf16[196,2048]{1,0:T(8,128)(2,1)}, f32[196,2048]{1,0:T(8,128)S(1)}, f32[196,2048]{1,0:T(8,128)S(1)}) fusion(f32[2048]{0:T(1024)} %bitcast.1695, bf16[196,512]{1,0:T(8,128)(2,1)} %reshape.3123, bf16[1,1,512,2048]{3,2,1,0:T(8,128)(2,1)} %get-tuple-element.343), kind=kOutput, calls=%fused_computation.791 | convolution fusion | flops 437534720 | bytes 6320128 | tf_op jit(solution)/shard_map/jvp()/dot_general | solution.py:55
  163.4 6.4 %pad_add_fusion.3 = f32[1,20,20,512]{3,2,1,0:T(8,128)S(1)} fusion(f32[1,14,14,512]{3,2,1,0:T(8,128)S(1)} %get-tuple-element.500, f32[1,14,14,512]{3,2,1,0:T(8,128)} %get-tuple-element.501, f32[1,14,14,512]{3,2,1,0:T(8,128)} %get-tuple-element.502, f32[1,14,14,512]{3,2,1,0:T(8,128)} %get-tuple-element.503, f32[1,14,14,512]{3,2,1,0:T(8,128)} %get-tuple-element.504, ...), kind=kLoop, calls=%fused_computation.962 | loop fusion | flops 8601600 | bytes 18079744 | tf_op jit(solution)/shard_map/transpose(jvp())/add_any | solution.py:29
  174.7 7.3 %multiply_convert_fusion.3 = (bf16[196,2048]{1,0:T(8,128)(2,1)S(1)}, f32[196,2048]{1,0:T(8,128)}, f32[196,2048]{1,0:T(8,128)}) fusion(f32[2048]{0:T(1024)} %bitcast.1696, bf16[196,512]{1,0:T(8,128)(2,1)} %reshape.3124, bf16[1,1,512,2048]{3,2,1,0:T(8,128)(2,1)} %get-tuple-element.343), kind=kOutput, calls=%fused_computation.790 | convolution fusion | flops 437534720 | bytes 6320128 | tf_op jit(solution)/shard_map/jvp()/dot_general | solution.py:55
  187.7 7.3 %multiply_convert_fusion.2 = (bf16[196,2048]{1,0:T(8,128)(2,1)S(1)}, f32[196,2048]{1,0:T(8,128)}, f32[196,2048]{1,0:T(8,128)}) fusion(f32[2048]{0:T(1024)} %bitcast.1697, bf16[196,512]{1,0:T(8,128)(2,1)} %reshape.3126, bf16[1,1,512,2048]{3,2,1,0:T(8,128)(2,1)} %get-tuple-element.343), kind=kOutput, calls=%fused_computation.789 | convolution fusion | flops 437534720 | bytes 6320128 | tf_op jit(solution)/shard_map/jvp()/dot_general | solution.py:55
  200.8 7.5 %multiply_convert_fusion.1 = (bf16[196,2048]{1,0:T(8,128)(2,1)S(1)}, f32[196,2048]{1,0:T(8,128)}, f32[196,2048]{1,0:T(8,128)}) fusion(f32[2048]{0:T(1024)} %bitcast.1698, bf16[196,512]{1,0:T(8,128)(2,1)} %reshape.3128, bf16[1,1,512,2048]{3,2,1,0:T(8,128)(2,1)} %get-tuple-element.343), kind=kOutput, calls=%fused_computation.788 | convolution fusion | flops 437534720 | bytes 6320128 | tf_op jit(solution)/shard_map/jvp()/dot_general | solution.py:55
  214.0 7.3 %multiply_convert_fusion = (bf16[196,2048]{1,0:T(8,128)(2,1)S(1)}, f32[196,2048]{1,0:T(8,128)}, f32[196,2048]{1,0:T(8,128)}) fusion(f32[2048]{0:T(1024)} %bitcast.1699, bf16[196,512]{1,0:T(8,128)(2,1)} %reshape.3130, bf16[1,1,512,2048]{3,2,1,0:T(8,128)(2,1)} %get-tuple-element.343), kind=kOutput, calls=%fused_computation.787 | convolution fusion | flops 437534720 | bytes 6320128 | tf_op jit(solution)/shard_map/jvp()/dot_general | solution.py:55
  235.0 4.3 fusion.1551
  260.9 6.3 %pad_add_fusion.2 = f32[1,20,20,512]{3,2,1,0:T(8,128)S(1)} fusion(f32[1,14,14,512]{3,2,1,0:T(8,128)S(1)} %get-tuple-element.455, f32[1,14,14,512]{3,2,1,0:T(8,128)S(1)} %get-tuple-element.456, f32[1,14,14,512]{3,2,1,0:T(8,128)} %get-tuple-element.457, f32[1,14,14,512]{3,2,1,0:T(8,128)} %get-tuple-element.458, f32[1,14,14,512]{3,2,1,0:T(8,128)} %get-tuple-element.459, ...), kind=kLoop, calls=%fused_computation.961 | loop fusion | flops 8601600 | bytes 18079744 | tf_op jit(solution)/shard_map/transpose(jvp())/add_any | solution.py:29
  271.9 3.9 collective-permute-done.5
  277.4 4.3 fusion.1550
  303.1 6.2 %pad_add_fusion.1 = f32[1,20,20,512]{3,2,1,0:T(8,128)S(1)} fusion(f32[1,14,14,512]{3,2,1,0:T(8,128)S(1)} %get-tuple-element.410, f32[1,14,14,512]{3,2,1,0:T(8,128)S(1)} %get-tuple-element.411, f32[1,14,14,512]{3,2,1,0:T(8,128)S(1)} %copy-done.64, f32[1,14,14,512]{3,2,1,0:T(8,128)} %get-tuple-element.413, f32[1,14,14,512]{3,2,1,0:T(8,128)} %get-tuple-element.414, ...), kind=kLoop, calls=%fused_computation.960 | loop fusion | flops 8601600 | bytes 18079744 | tf_op jit(solution)/shard_map/transpose(jvp())/add_any | solution.py:29
  319.5 4.3 fusion.1549
  343.6 6.2 %pad_add_fusion = f32[1,20,20,512]{3,2,1,0:T(8,128)S(1)} fusion(f32[1,14,14,512]{3,2,1,0:T(8,128)S(1)} %get-tuple-element.365, f32[1,14,14,512]{3,2,1,0:T(8,128)S(1)} %get-tuple-element.366, f32[1,14,14,512]{3,2,1,0:T(8,128)S(1)} %get-tuple-element.367, f32[1,14,14,512]{3,2,1,0:T(8,128)S(1)} %copy-done.63, f32[1,14,14,512]{3,2,1,0:T(8,128)} %get-tuple-element.369, ...), kind=kLoop, calls=%fused_computation.959 | loop fusion | flops 8601600 | bytes 18079744 | tf_op jit(solution)/shard_map/transpose(jvp())/add_any | solution.py:29
  354.4 3.9 collective-permute-done.7
  359.2 4.3 fusion.1548
  370.8 5.9 fusion.1
  381.7 4.2 bitcast_subtract_fusion
  386.0 5.2 reshape.3133
  398.4 5.4 gather_fusion
  403.8 6.3 %fusion = bf16[32,512,128]{2,1,0:T(8,128)(2,1)} fusion(bf16[32,512,128]{2,1,0:T(8,128)(2,1)} %gather_fusion, pred[32]{0:T(512)(128)(4,1)S(1)} %copy-done.561, pred[32]{0:T(512)(128)(4,1)S(1)} %copy-done.560), kind=kLoop, calls=%fused_computation.629 | loop fusion | flops 4194304 | bytes 8388672 | tf_op jit(solution)/shard_map/convert_element_type | solution.py:106
  410.1 8.6 %all-to-all-start = ((bf16[32,512,128]{2,1,0:T(8,128)(2,1)}), bf16[32,512,128]{2,1,0:T(8,128)(2,1)}, u32[]{:S(2)}, u32[]{:S(2)}) async-start(bf16[32,512,128]{2,1,0:T(8,128)(2,1)} %fusion), calls=%async_computation | async-start | bytes 8388608 | tf_op jit(solution)/shard_map/all_to_all | solution.py:105
  430.0 42.1 %all-to-all-done = bf16[32,512,128]{2,1,0:T(8,128)(2,1)} async-done(((bf16[32,512,128]{2,1,0:T(8,128)(2,1)}), bf16[32,512,128]{2,1,0:T(8,128)(2,1)}, u32[]{:S(2)}, u32[]{:S(2)}) %all-to-all-start) | async-done | bytes 4194336 | tf_op jit(solution)/shard_map/all_to_all | solution.py:105
  472.1 6.4 %convert_element_type.646 = f32[32,512,128]{2,1,0:T(8,128)} convert(bf16[32,512,128]{2,1,0:T(8,128)(2,1)} %all-to-all-done) | non-fusion elementwise | flops 2097152 | bytes 12582912 | tf_op jit(solution)/shard_map/convert_element_type | solution.py:107
  478.5 7.8 %gather_fusion.1 = f32[32,512,128]{2,1,0:T(8,128)} fusion(f32[32,512,128]{2,1,0:T(8,128)} %convert_element_type.646, s32[1024]{0:T(1024)} %pad_clamp_fusion), kind=kCustom, calls=%fused_computation.1.clone | custom fusion | bytes 16777344 | tf_op jit(solution)/shard_map/jit(_take)/gather | solution.py:109
  486.4 6.9 %select_select_fusion = f32[32,512,128]{2,1,0:T(8,128)S(1)} fusion(f32[32,512,128]{2,1,0:T(8,128)} %gather_fusion.1, pred[32]{0:T(512)(128)(4,1)S(1)} %copy-done.545, pred[32]{0:T(512)(128)(4,1)S(1)} %copy-done.544, f32[16,512,128]{2,1,0:T(8,128)} %bitcast.611, f32[16,512,128]{2,1,0:T(8,128)} %bitcast.608), kind=kLoop, calls=%fused_computation.627 | loop fusion | flops 6291456 | bytes 25165888 | tf_op jit(solution)/shard_map/jit(_where)/select_n | solution.py:108
  498.0 4.0 copy.87
  504.9 6.8 %fusion.153 = f32[196,512]{1,0:T(8,128)S(1)} fusion(bf16[256,8,4,128]{3,2,1,0:T(4,128)(2,1)} %bitcast.617, bf16[196,512]{1,0:T(8,128)(2,1)S(1)} %reshape.3140, bf16[512,2048]{0,1:T(8,128)(2,1)} %bitcast.621, f32[2048]{0:T(1024)S(1)} %multiply_subtract_fusion.1, f32[512]{0:T(512)S(1)} %multiply_subtract_fusion.2), kind=kOutput, calls=%fused_computation.934 | convolution fusion | flops 848676864 | bytes 4806656 | tf_op jit(solution)/shard_map/dot_general | solution.py:58
  511.8 4.1 collective-permute-start.8
  515.9 4.0 collective-permute-done.8
  524.6 6.9 %fusion.156 = f32[196,512]{1,0:T(8,128)} fusion(bf16[256,8,4,128]{3,2,1,0:T(4,128)(2,1)S(1)} %bitcast.618, bf16[196,512]{1,0:T(8,128)(2,1)S(1)} %reshape.3142, bf16[512,2048]{0,1:T(8,128)(2,1)} %bitcast.622, f32[2048]{0:T(1024)S(1)} %multiply_subtract_fusion.1, f32[512]{0:T(512)S(1)} %multiply_subtract_fusion.2), kind=kOutput, calls=%fused_computation.935 | convolution fusion | flops 848676864 | bytes 4806656 | tf_op jit(solution)/shard_map/dot_general | solution.py:58
  533.6 4.5 collective-permute-start.9
  546.4 6.9 %fusion.159 = f32[196,512]{1,0:T(8,128)} fusion(bf16[256,8,4,128]{3,2,1,0:T(4,128)(2,1)S(1)} %bitcast.619, bf16[196,512]{1,0:T(8,128)(2,1)S(1)} %reshape.3144, bf16[512,2048]{0,1:T(8,128)(2,1)} %bitcast.623, f32[2048]{0:T(1024)S(1)} %copy-done.535, f32[512]{0:T(512)S(1)} %copy-done.557), kind=kOutput, calls=%fused_computation.936 | convolution fusion | flops 848676864 | bytes 4806656 | tf_op jit(solution)/shard_map/dot_general | solution.py:58
  555.7 4.1 collective-permute-start.10
  559.8 6.8 %copy.85 = f32[4,4,512,128]{3,0,2,1:T(4,128)} copy(f32[4,4,512,128]{3,2,1,0:T(8,128)} %bitcast.613) | data formatting | bytes 8388608 | tf_op jit(solution)/shard_map/reshape | solution.py:113
  566.6 5.5 broadcast_in_dim_reshape.7
  572.1 5.3 copy.36
  577.7 5.3 copy.39
  587.7 6.9 %fusion.162 = f32[196,512]{1,0:T(8,128)} fusion(bf16[256,8,4,128]{3,2,1,0:T(4,128)(2,1)S(1)} %bitcast.620, bf16[196,512]{1,0:T(8,128)(2,1)S(1)} %reshape.3146, bf16[512,2048]{0,1:T(8,128)(2,1)} %bitcast.624, f32[2048]{0:T(1024)} %copy-done.534, f32[512]{0:T(512)} %copy-done.556), kind=kOutput, calls=%fused_computation.937 | convolution fusion | flops 848676864 | bytes 4806656 | tf_op jit(solution)/shard_map/dot_general | solution.py:58
  (1376 shorter events, 275.5 us)
Async XLA Ops:
  26.3 11.5 %collective-permute-start = (bf16[1,14,14,512]{3,2,1,0:T(8,128)(2,1)}, bf16[1,14,14,512]{3,2,1,0:T(8,128)(2,1)}, u32[]{:S(2)}, u32[]{:S(2)}) collective-permute-start(bf16[1,14,14,512]{3,2,1,0:T(8,128)(2,1)} %add_convert_fusion.19), channel_id=1, source_target_pairs={{0,1},{1,2},{2,3},{4,5},{5,6},{6,7},{8,9},{9,10},{10,11},{12,13},{... | collective-permute-start | bytes 602120 | tf_op jit(solution)/shard_map/ppermute | solution.py:16
  53.6 9.0 %collective-permute-start.1 = (bf16[1,14,14,512]{3,2,1,0:T(8,128)(2,1)S(1)}, bf16[1,14,14,512]{3,2,1,0:T(8,128)(2,1)S(1)}, u32[]{:S(2)}, u32[]{:S(2)}) collective-permute-start(bf16[1,14,14,512]{3,2,1,0:T(8,128)(2,1)S(1)} %add_convert_fusion.17), channel_id=1, source_target_pairs={{0,1},{1,2},{2,3},{4,5},{5,6},{6,7},{8,9},{9,10},{10,11},{12,13},{... | collective-permute-start | bytes 602120 | tf_op jit(solution)/shard_map/ppermute | solution.py:16
  77.8 8.0 %collective-permute-start.2 = (bf16[1,14,14,512]{3,2,1,0:T(8,128)(2,1)S(1)}, bf16[1,14,14,512]{3,2,1,0:T(8,128)(2,1)S(1)}, u32[]{:S(2)}, u32[]{:S(2)}) collective-permute-start(bf16[1,14,14,512]{3,2,1,0:T(8,128)(2,1)S(1)} %add_convert_fusion.15), channel_id=1, source_target_pairs={{0,1},{1,2},{2,3},{4,5},{5,6},{6,7},{8,9},{9,10},{10,11},{12,13},{... | collective-permute-start | bytes 602120 | tf_op jit(solution)/shard_map/ppermute | solution.py:16
  101.5 7.9 %collective-permute-start.3 = (bf16[1,14,14,512]{3,2,1,0:T(8,128)(2,1)S(1)}, bf16[1,14,14,512]{3,2,1,0:T(8,128)(2,1)S(1)}, u32[]{:S(2)}, u32[]{:S(2)}) collective-permute-start(bf16[1,14,14,512]{3,2,1,0:T(8,128)(2,1)S(1)} %add_convert_fusion.13), channel_id=1, source_target_pairs={{0,1},{1,2},{2,3},{4,5},{5,6},{6,7},{8,9},{9,10},{10,11},{12,13},{... | collective-permute-start | bytes 602120 | tf_op jit(solution)/shard_map/ppermute | solution.py:16
  170.9 59.3 %collective-permute-start.4 = (bf16[1,14,14,512]{3,2,1,0:T(8,128)(2,1)}, bf16[1,14,14,512]{3,2,1,0:T(8,128)(2,1)}, u32[]{:S(2)}, u32[]{:S(2)}) collective-permute-start(bf16[1,14,14,512]{3,2,1,0:T(8,128)(2,1)} %fusion.1224), channel_id=1, source_target_pairs={{1,0},{2,1},{3,2},{5,4},{6,5},{7,6},{9,8},{10,9},{11,10},{13,12},{... | collective-permute-start | bytes 602120 | tf_op jit(solution)/shard_map/ppermute | solution.py:16
  267.7 8.0 %collective-permute-start.5 = (bf16[1,14,14,512]{3,2,1,0:T(8,128)(2,1)S(1)}, bf16[1,14,14,512]{3,2,1,0:T(8,128)(2,1)S(1)}, u32[]{:S(2)}, u32[]{:S(2)}) collective-permute-start(bf16[1,14,14,512]{3,2,1,0:T(8,128)(2,1)S(1)} %fusion.441), channel_id=1, source_target_pairs={{1,0},{2,1},{3,2},{5,4},{6,5},{7,6},{9,8},{10,9},{11,10},{13,12},{... | collective-permute-start | bytes 602120 | tf_op jit(solution)/shard_map/ppermute | solution.py:16
  309.8 8.0 %collective-permute-start.6 = (bf16[1,14,14,512]{3,2,1,0:T(8,128)(2,1)S(1)}, bf16[1,14,14,512]{3,2,1,0:T(8,128)(2,1)S(1)}, u32[]{:S(2)}, u32[]{:S(2)}) collective-permute-start(bf16[1,14,14,512]{3,2,1,0:T(8,128)(2,1)S(1)} %fusion.443), channel_id=1, source_target_pairs={{1,0},{2,1},{3,2},{5,4},{6,5},{7,6},{9,8},{10,9},{11,10},{13,12},{... | collective-permute-start | bytes 602120 | tf_op jit(solution)/shard_map/ppermute | solution.py:16
  350.2 8.0 %collective-permute-start.7 = (bf16[1,14,14,512]{3,2,1,0:T(8,128)(2,1)S(1)}, bf16[1,14,14,512]{3,2,1,0:T(8,128)(2,1)S(1)}, u32[]{:S(2)}, u32[]{:S(2)}) collective-permute-start(bf16[1,14,14,512]{3,2,1,0:T(8,128)(2,1)S(1)} %fusion.445), channel_id=1, source_target_pairs={{1,0},{2,1},{3,2},{5,4},{6,5},{7,6},{9,8},{10,9},{11,10},{13,12},{... | collective-permute-start | bytes 602120 | tf_op jit(solution)/shard_map/ppermute | solution.py:16
  410.1 62.0 %all-to-all-start = ((bf16[32,512,128]{2,1,0:T(8,128)(2,1)}), bf16[32,512,128]{2,1,0:T(8,128)(2,1)}, u32[]{:S(2)}, u32[]{:S(2)}) async-start(bf16[32,512,128]{2,1,0:T(8,128)(2,1)} %fusion), calls=%async_computation | async-start | bytes 8388608 | tf_op jit(solution)/shard_map/all_to_all | solution.py:105
  424.9 95.0 %copy-start.372 = (f32[1,1,512]{2,1,0:T(1,128)}, f32[1,1,512]{2,1,0:T(1,128)S(1)}, u32[]{:S(2)}) copy-start(f32[1,1,512]{2,1,0:T(1,128)S(1)} %get-tuple-element.556) | copy-start | bytes 6148
  425.0 95.0 %copy-start.374 = (f32[1,1,512]{2,1,0:T(1,128)}, f32[1,1,512]{2,1,0:T(1,128)S(1)}, u32[]{:S(2)}) copy-start(f32[1,1,512]{2,1,0:T(1,128)S(1)} %get-tuple-element.557) | copy-start | bytes 6148
  425.0 95.0 %copy-start.376 = (f32[1,1,512]{2,1,0:T(1,128)}, f32[1,1,512]{2,1,0:T(1,128)S(1)}, u32[]{:S(2)}) copy-start(f32[1,1,512]{2,1,0:T(1,128)S(1)} %get-tuple-element.558) | copy-start | bytes 6148
  425.0 95.0 %copy-start.379 = (f32[1,1,512]{2,1,0:T(1,128)}, f32[1,1,512]{2,1,0:T(1,128)S(1)}, u32[]{:S(2)}) copy-start(f32[1,1,512]{2,1,0:T(1,128)S(1)} %get-tuple-element.559) | copy-start | bytes 6148
  425.0 95.0 %copy-start.382 = (f32[1,1,512]{2,1,0:T(1,128)}, f32[1,1,512]{2,1,0:T(1,128)S(1)}, u32[]{:S(2)}) copy-start(f32[1,1,512]{2,1,0:T(1,128)S(1)} %get-tuple-element.560) | copy-start | bytes 6148
  425.0 95.0 %copy-start.385 = (f32[1,1,512]{2,1,0:T(1,128)}, f32[1,1,512]{2,1,0:T(1,128)S(1)}, u32[]{:S(2)}) copy-start(f32[1,1,512]{2,1,0:T(1,128)S(1)} %get-tuple-element.561) | copy-start | bytes 6148
  425.0 95.0 %copy-start.388 = (f32[1,1,512]{2,1,0:T(1,128)}, f32[1,1,512]{2,1,0:T(1,128)S(1)}, u32[]{:S(2)}) copy-start(f32[1,1,512]{2,1,0:T(1,128)S(1)} %get-tuple-element.562) | copy-start | bytes 6148
  425.0 95.0 %copy-start.391 = (f32[1,1,512]{2,1,0:T(1,128)}, f32[1,1,512]{2,1,0:T(1,128)S(1)}, u32[]{:S(2)}) copy-start(f32[1,1,512]{2,1,0:T(1,128)S(1)} %get-tuple-element.563) | copy-start | bytes 6148
  425.0 95.0 %copy-start.394 = (f32[1,1,512]{2,1,0:T(1,128)}, f32[1,1,512]{2,1,0:T(1,128)S(1)}, u32[]{:S(2)}) copy-start(f32[1,1,512]{2,1,0:T(1,128)S(1)} %get-tuple-element.564) | copy-start | bytes 6148
  425.0 95.0 %copy-start.397 = (f32[1,1,512]{2,1,0:T(1,128)}, f32[1,1,512]{2,1,0:T(1,128)S(1)}, u32[]{:S(2)}) copy-start(f32[1,1,512]{2,1,0:T(1,128)S(1)} %get-tuple-element.565) | copy-start | bytes 6148
  425.0 95.0 %copy-start.400 = (f32[1,1,512]{2,1,0:T(1,128)}, f32[1,1,512]{2,1,0:T(1,128)S(1)}, u32[]{:S(2)}) copy-start(f32[1,1,512]{2,1,0:T(1,128)S(1)} %get-tuple-element.566) | copy-start | bytes 6148
  425.1 95.0 %copy-start.403 = (f32[1,1,512]{2,1,0:T(1,128)}, f32[1,1,512]{2,1,0:T(1,128)S(1)}, u32[]{:S(2)}) copy-start(f32[1,1,512]{2,1,0:T(1,128)S(1)} %get-tuple-element.567) | copy-start | bytes 6148
  425.1 95.0 %copy-start.406 = (f32[1,1,512]{2,1,0:T(1,128)}, f32[1,1,512]{2,1,0:T(1,128)S(1)}, u32[]{:S(2)}) copy-start(f32[1,1,512]{2,1,0:T(1,128)S(1)} %get-tuple-element.568) | copy-start | bytes 6148
  425.1 94.9 %copy-start.409 = (f32[1,1,512]{2,1,0:T(1,128)}, f32[1,1,512]{2,1,0:T(1,128)S(1)}, u32[]{:S(2)}) copy-start(f32[1,1,512]{2,1,0:T(1,128)S(1)} %get-tuple-element.569) | copy-start | bytes 6148
  425.1 94.9 %copy-start.412 = (f32[1,1,512]{2,1,0:T(1,128)}, f32[1,1,512]{2,1,0:T(1,128)S(1)}, u32[]{:S(2)}) copy-start(f32[1,1,512]{2,1,0:T(1,128)S(1)} %get-tuple-element.570) | copy-start | bytes 6148
  425.1 94.9 %copy-start.415 = (f32[1,1,512]{2,1,0:T(1,128)}, f32[1,1,512]{2,1,0:T(1,128)S(1)}, u32[]{:S(2)}) copy-start(f32[1,1,512]{2,1,0:T(1,128)S(1)} %get-tuple-element.571) | copy-start | bytes 6148
  425.1 94.9 %copy-start.418 = (f32[1,1,512]{2,1,0:T(1,128)}, f32[1,1,512]{2,1,0:T(1,128)S(1)}, u32[]{:S(2)}) copy-start(f32[1,1,512]{2,1,0:T(1,128)S(1)} %get-tuple-element.572) | copy-start | bytes 6148
  425.2 94.9 %copy-start.421 = (f32[1,1,512]{2,1,0:T(1,128)}, f32[1,1,512]{2,1,0:T(1,128)S(1)}, u32[]{:S(2)}) copy-start(f32[1,1,512]{2,1,0:T(1,128)S(1)} %get-tuple-element.573) | copy-start | bytes 6148
  425.2 94.9 %copy-start.424 = (f32[1,1,512]{2,1,0:T(1,128)}, f32[1,1,512]{2,1,0:T(1,128)S(1)}, u32[]{:S(2)}) copy-start(f32[1,1,512]{2,1,0:T(1,128)S(1)} %get-tuple-element.574) | copy-start | bytes 6148
  425.2 94.9 %copy-start.427 = (f32[1,1,512]{2,1,0:T(1,128)}, f32[1,1,512]{2,1,0:T(1,128)S(1)}, u32[]{:S(2)}) copy-start(f32[1,1,512]{2,1,0:T(1,128)S(1)} %get-tuple-element.575) | copy-start | bytes 6148
  425.2 94.9 %copy-start.430 = (f32[1,1,512]{2,1,0:T(1,128)}, f32[1,1,512]{2,1,0:T(1,128)S(1)}, u32[]{:S(2)}) copy-start(f32[1,1,512]{2,1,0:T(1,128)S(1)} %get-tuple-element.576) | copy-start | bytes 6148
  425.2 94.9 %copy-start.433 = (f32[1,1,512]{2,1,0:T(1,128)}, f32[1,1,512]{2,1,0:T(1,128)S(1)}, u32[]{:S(2)}) copy-start(f32[1,1,512]{2,1,0:T(1,128)S(1)} %get-tuple-element.577) | copy-start | bytes 6148
  425.2 94.9 %copy-start.436 = (f32[1,1,512]{2,1,0:T(1,128)}, f32[1,1,512]{2,1,0:T(1,128)S(1)}, u32[]{:S(2)}) copy-start(f32[1,1,512]{2,1,0:T(1,128)S(1)} %get-tuple-element.578) | copy-start | bytes 6148
  425.2 94.9 %copy-start.439 = (f32[1,1,512]{2,1,0:T(1,128)}, f32[1,1,512]{2,1,0:T(1,128)S(1)}, u32[]{:S(2)}) copy-start(f32[1,1,512]{2,1,0:T(1,128)S(1)} %get-tuple-element.579) | copy-start | bytes 6148
  425.2 94.9 %copy-start.442 = (f32[1,1,512]{2,1,0:T(1,128)}, f32[1,1,512]{2,1,0:T(1,128)S(1)}, u32[]{:S(2)}) copy-start(f32[1,1,512]{2,1,0:T(1,128)S(1)} %get-tuple-element.580) | copy-start | bytes 6148
  425.2 94.9 %copy-start.445 = (f32[1,1,512]{2,1,0:T(1,128)}, f32[1,1,512]{2,1,0:T(1,128)S(1)}, u32[]{:S(2)}) copy-start(f32[1,1,512]{2,1,0:T(1,128)S(1)} %get-tuple-element.581) | copy-start | bytes 6148
  425.2 94.9 %copy-start.448 = (f32[1,1,512]{2,1,0:T(1,128)}, f32[1,1,512]{2,1,0:T(1,128)S(1)}, u32[]{:S(2)}) copy-start(f32[1,1,512]{2,1,0:T(1,128)S(1)} %get-tuple-element.582) | copy-start | bytes 6148
  425.3 94.9 %copy-start.451 = (f32[1,1,512]{2,1,0:T(1,128)}, f32[1,1,512]{2,1,0:T(1,128)S(1)}, u32[]{:S(2)}) copy-start(f32[1,1,512]{2,1,0:T(1,128)S(1)} %get-tuple-element.583) | copy-start | bytes 6148
  425.3 94.9 %copy-start.454 = (f32[1,1,512]{2,1,0:T(1,128)}, f32[1,1,512]{2,1,0:T(1,128)S(1)}, u32[]{:S(2)}) copy-start(f32[1,1,512]{2,1,0:T(1,128)S(1)} %get-tuple-element.584) | copy-start | bytes 6148
  425.3 94.9 %copy-start.457 = (f32[1,1,512]{2,1,0:T(1,128)}, f32[1,1,512]{2,1,0:T(1,128)S(1)}, u32[]{:S(2)}) copy-start(f32[1,1,512]{2,1,0:T(1,128)S(1)} %get-tuple-element.585) | copy-start | bytes 6148
  425.3 94.9 %copy-start.460 = (f32[1,1,512]{2,1,0:T(1,128)}, f32[1,1,512]{2,1,0:T(1,128)S(1)}, u32[]{:S(2)}) copy-start(f32[1,1,512]{2,1,0:T(1,128)S(1)} %get-tuple-element.586) | copy-start | bytes 6148
  425.3 94.9 %copy-start.463 = (f32[1,1,512]{2,1,0:T(1,128)}, f32[1,1,512]{2,1,0:T(1,128)S(1)}, u32[]{:S(2)}) copy-start(f32[1,1,512]{2,1,0:T(1,128)S(1)} %get-tuple-element.587) | copy-start | bytes 6148
  429.4 94.9 %copy-start.466 = (f32[512]{0:T(512)}, f32[512]{0:T(512)S(1)}, u32[]{:S(2)}) copy-start(f32[512]{0:T(512)S(1)} %multiply_subtract_fusion.4) | copy-start | bytes 6148
  429.5 94.8 %copy-start.471 = (f32[512]{0:T(512)}, f32[512]{0:T(512)S(1)}, u32[]{:S(2)}) copy-start(f32[512]{0:T(512)S(1)} %multiply_subtract_fusion.3) | copy-start | bytes 6148
  429.9 94.6 %copy-start.556 = (f32[512]{0:T(512)}, f32[512]{0:T(512)S(1)}, u32[]{:S(2)}) copy-start(f32[512]{0:T(512)S(1)} %multiply_subtract_fusion.2) | copy-start | bytes 6148
  430.0 94.6 %copy-start.534 = (f32[2048]{0:T(1024)}, f32[2048]{0:T(1024)S(1)}, u32[]{:S(2)}) copy-start(f32[2048]{0:T(1024)S(1)} %multiply_subtract_fusion.1) | copy-start | bytes 24580
  511.8 8.0 %collective-permute-start.8 = (bf16[1,14,14,512]{3,2,1,0:T(8,128)(2,1)S(1)}, bf16[1,14,14,512]{3,2,1,0:T(8,128)(2,1)S(1)}, u32[]{:S(2)}, u32[]{:S(2)}) collective-permute-start(bf16[1,14,14,512]{3,2,1,0:T(8,128)(2,1)S(1)} %add_convert_fusion.6), channel_id=1, source_target_pairs={{0,1},{1,2},{2,3},{4,5},{5,6},{6,7},{8,9},{9,10},{10,11},{12,13},{... | collective-permute-start | bytes 602120 | tf_op jit(solution)/shard_map/ppermute | solution.py:16
  533.6 8.0 %collective-permute-start.9 = (bf16[1,14,14,512]{3,2,1,0:T(8,128)(2,1)S(1)}, bf16[1,14,14,512]{3,2,1,0:T(8,128)(2,1)S(1)}, u32[]{:S(2)}, u32[]{:S(2)}) collective-permute-start(bf16[1,14,14,512]{3,2,1,0:T(8,128)(2,1)S(1)} %add_convert_fusion.4), channel_id=1, source_target_pairs={{0,1},{1,2},{2,3},{4,5},{5,6},{6,7},{8,9},{9,10},{10,11},{12,13},{... | collective-permute-start | bytes 602120 | tf_op jit(solution)/shard_map/ppermute | solution.py:16
  555.7 27.3 %collective-permute-start.10 = (bf16[1,14,14,512]{3,2,1,0:T(8,128)(2,1)}, bf16[1,14,14,512]{3,2,1,0:T(8,128)(2,1)S(1)}, u32[]{:S(2)}, u32[]{:S(2)}) collective-permute-start(bf16[1,14,14,512]{3,2,1,0:T(8,128)(2,1)} %add_convert_fusion.2), channel_id=1, source_target_pairs={{0,1},{1,2},{2,3},{4,5},{5,6},{6,7},{8,9},{9,10},{10,11},{12,13},{... | collective-permute-start | bytes 602120 | tf_op jit(solution)/shard_map/ppermute | solution.py:16
  (532 other events, 3512.0 us)
where the time goes:
time: 606 us; the launch traced here: 597 us
  other arithmetic  202 us (33%)
  matrix products  157 us (26%)
  local copies, waits for them, and re-layouts  113 us (19%)
  waiting for transfers between devices  72.5 us (12%)
  starting transfers between devices  43.7 us (7%)
  between operations  9.2 us (2%)
    dot_general x23, matrix products, block(): jnp.dot(hidden, second_weight, preferred_element_type=jnp.float32)  96.5 us
    dot_general x15, matrix products, block(): jnp.dot(rows, first_weight, preferred_element_type=jnp.float32) + first_bias  60.1 us
    reduce_sum x13, other arithmetic, block(): center = jnp.mean(spread, axis=-1, keepdims=True)  50.7 us
    all_to_all x1, waiting for transfers between devices, shuffle(): lax.all_to_all(outgoing.astype(jnp.bfloat16), 'member', split_axis=0, con...  42.1 us
    ppermute x11, starting transfers between devices, from_behind(): lax.ppermute(value, axis, [(source, source + steps) for source in range(f...  35.1 us
    ppermute x11, waiting for transfers between devices, from_behind(): lax.ppermute(value, axis, [(source, source + steps) for source in range(f...  30.3 us
    reduce_sum x15, other arithmetic, depthwise(): kernel[row_off, col_off]  29.4 us
    add_any x4, other arithmetic, depthwise(): padded[:, row_off:row_off + height, col_off:col_off + width, :]  25 us
  transfers between devices with their start and end apart: 12, of which 9 were waited for; matrix products, arithmetic and copies ran while one was open for 17% of the time, Pallas kernels for 0%

commit v1 on v0

v1 whole, which is shorter than its diff:
```python
import functools

import jax
import jax.numpy as jnp
from jax import lax
from jax.experimental import pallas as pl
from jax.experimental.pallas import tpu as pltpu
from jax.sharding import PartitionSpec as P

MESH = pl.DeviceIdType.MESH
BF = jnp.bfloat16
F32 = jnp.float32
S = 14
W = 16
R = S * W
D = 512
HID = 2048
LANE = 128
TILE = 128
CH = 512
learning_rate = 0.001
norm_epsilon = 1e-06


def dot(a, b, ca, cb):
    return lax.dot_general(a, b, (((ca,), (cb,)), ((), ())), preferred_element_type=F32)


def loop(n, body):
    lax.fori_loop(0, n, lambda i, c: (body(i), c)[1], 0)


def lanes_of(c):
    return pl.ds(pl.multiple_of(c * LANE, LANE), LANE)


def shifted(x, d):
    col = lax.broadcasted_iota(jnp.int32, (R, LANE), 0) % W + d
    moved = x if d == 0 else pltpu.roll(x, (-d) % R, 0)
    return jnp.where((col >= 0) & (col < S), moved, 0.0).reshape(S, W, LANE)


def fill_shifts(x, sh, lanes):
    for dj in range(7):
        sh[dj, 3 : 3 + S, :, lanes] = shifted(x, dj - 3)


def zero_borders(sh):
    zeros = jnp.zeros((7, 3, W, D), F32)
    sh[:, 0:3] = zeros
    sh[:, 3 + S :] = zeros


def taps(sh, k, lanes, start, flip):
    total = start
    for di in range(7):
        for dj in range(7):
            ki, kj = (6 - di, 6 - dj) if flip else (di, dj)
            weight = k[ki, kj : kj + 1, lanes].reshape(1, 1, LANE)
            total = total + weight * sh[dj, di : di + S, :, lanes]
    return total


def gelu_parts(x):
    t = 1.0 / (1.0 + 0.23164189 * jnp.abs(x))
    e = jnp.exp(-0.5 * (x * x))
    poly = t * (
        0.127414796
        + t * (-0.142248368 + t * (0.7107068705 + t * (-0.7265760135 + t * 0.5307027145)))
    )
    q = poly * e
    return jnp.where(x < 0.0, q, 1.0 - q), e


def forward(x, sh, conv, k, kb, gain, nb, w1, b1, w2, b2, ls, u, h, n, out, keep):
    def conv_lanes(c):
        lanes = lanes_of(c)
        fill_shifts(x[:, :, lanes].reshape(R, LANE), sh, lanes)
        start = jnp.zeros((S, W, LANE), F32) + kb[:, lanes].reshape(1, 1, LANE)
        conv[:, lanes] = taps(sh, k, lanes, start, False).reshape(R, LANE)

    loop(D // LANE, conv_lanes)

    def norm_rows(i):
        rows = pl.ds(pl.multiple_of(i * 32, 32), 32)
        c = conv[rows, :]
        off = c - jnp.mean(c, axis=-1, keepdims=True)
        var = jnp.mean(off * off, axis=-1, keepdims=True)
        rstd = lax.rsqrt(var + norm_epsilon)
        hat = off * rstd
        n[rows, :] = (hat * gain[...] + nb[...]).astype(BF)
        if keep is not None:
            keep[0][rows, :] = hat
            keep[1][rows, :] = rstd

    loop(R // 32, norm_rows)

    for c in range(HID // CH):
        cols = pl.ds(c * CH, CH)
        u[:, cols] = dot(n[...], w1[:, cols], 1, 0)

        def act(i, cols=cols):
            rows = pl.ds(pl.multiple_of(i * 16, 16), 16)
            a = u[rows, cols] + b1[:, cols]
            phi, e = gelu_parts(a)
            h[rows, cols] = (a * phi).astype(BF)
            if keep is not None:
                keep[2][rows, cols] = phi + a * e * 0.3989422804014327

        loop(R // 16, act)
    total = dot(h[...], w2[...], 1, 0)
    mixed = total + b2[...]
    if keep is not None:
        keep[3][...] = mixed
    flat = x[...].reshape(R, D)
    out(flat + ls[...] * mixed)


def unpadded(values):
    col = lax.broadcasted_iota(jnp.int32, (R, D), 0) % W
    return jnp.where(col < S, values, 0.0)


def neighbours_ready():
    s = lax.axis_index("section")
    count = lax.axis_size("section")
    barrier = pltpu.get_barrier_semaphore()
    for other in (lax.rem(s + 1, count), lax.rem(s + count - 1, count)):
        pl.semaphore_signal(barrier, inc=1, device_id={"section": other}, device_id_type=MESH)
    pl.semaphore_wait(barrier, 2)


def to_section(src, dst, send, recv, section):
    return pltpu.make_async_remote_copy(
        src_ref=src,
        dst_ref=dst,
        send_sem=send,
        recv_sem=recv,
        device_id={"section": section},
        device_id_type=MESH,
    )


def train_kernel(
    inputs, cot, k, kb, gain, nb, w1, b1, w2, b2, ls,
    o_k, o_kb, o_gain, o_nb, o_w1, o_b1, o_w2, o_b2, o_ls, o_tiles,
    w1b, w2b, x, sh, shd, conv, xhat, rstd, nrm, u, h, gp, mixed, dmb, du, dc, g,
    gk, gkb, ggain, gnb, gb1, gb2, gls,
    fsend, frecv, bsend, brecv, f_s, f_r, b_s, b_r,
):
    s = lax.axis_index("section")
    last = lax.axis_size("section") - 1
    up = jnp.minimum(s + 1, last)
    down = jnp.maximum(s - 1, 0)
    neighbours_ready()

    def cast(i):
        rows = pl.ds(pl.multiple_of(i * 32, 32), 32)
        w1b[rows, :] = w1[rows, :].astype(BF)
        rows = pl.ds(pl.multiple_of(i * 128, 128), 128)
        w2b[rows, :] = w2[rows, :].astype(BF)

    loop(16, cast)
    for ref in (gk, gkb, ggain, gnb, gb1, gb2, gls):
        ref[...] = jnp.zeros_like(ref)
    for j in range(2):
        zero_borders(sh.at[j])
    zero_borders(shd)

    def take(j, first, given, arrived, wait, dst):
        @pl.when(first)
        def _():
            dst[:, S:W, :] = jnp.zeros((S, W - S, D), F32)
            dst[:, 0:S, :] = given[j].astype(F32)

        @pl.when(jnp.logical_not(first))
        def _():
            wait()
            dst[...] = arrived[j].astype(F32)

    def fwd(j):
        rows = pl.ds(pl.multiple_of(j * R, R), R)
        copy = to_section(fsend.at[j], frecv.at[j], f_s.at[j], f_r.at[j], up)
        take(j, s == 0, inputs, frecv, copy.wait_recv, x.at[j])

        def out(values):
            @pl.when(s < last)
            def _():
                fsend[j] = unpadded(values).astype(BF).reshape(S, W, D)
                copy.start()

        forward(
            x.at[j], sh.at[j], conv, k, kb, gain, nb, w1b, b1, w2b, b2, ls,
            u, h.at[rows, :], nrm.at[rows, :], out,
            (xhat.at[j], rstd.at[j], gp.at[j], mixed.at[j]),
        )

    loop(2, fwd)

    def kernel_grad(j):
        def per_lanes(c):
            lanes = lanes_of(c)
            d = dc[j, :, :, lanes]
            for di in range(7):
                for dj in range(7):
                    prod = jnp.sum(d * sh[j, dj, di : di + S, :, lanes], axis=0)
                    gk[di, dj : dj + 1, lanes] += jnp.sum(prod, axis=0, keepdims=True)

        loop(D // LANE, per_lanes)

    def bwd(j):
        base = pl.multiple_of(j * R, R)
        rows = pl.ds(base, R)
        copy = to_section(bsend.at[j], brecv.at[j], b_s.at[j], b_r.at[j], down)
        take(j, s == last, cot, brecv, copy.wait_recv, g)

        flat = g[...].reshape(R, D)
        dm = flat * ls[...]
        dmb[rows, :] = dm.astype(BF)
        gb2[...] += jnp.sum(dm, axis=0, keepdims=True)
        gls[...] += jnp.sum(flat * mixed[j], axis=0, keepdims=True)
        for c in range(HID // CH):
            cols = pl.ds(c * CH, CH)
            u[:, cols] = dot(dmb[rows, :], w2b[cols, :], 1, 1)

            def act(i, carry, cols=cols):
                r = pl.ds(pl.multiple_of(i * 16, 16), 16)
                a = u[r, cols].astype(BF).astype(F32) * gp[j, r, cols]
                du[pl.ds(pl.multiple_of(base + i * 16, 16), 16), cols] = a.astype(BF)
                return carry + jnp.sum(a.reshape(2, 8, CH), axis=0)

            part = lax.fori_loop(0, R // 16, act, jnp.zeros((8, CH), F32))
            gb1[:, cols] += jnp.sum(part, axis=0, keepdims=True)
        conv[...] = dot(du[rows, :], w1b[...], 1, 1)

        def norm_rows(i, carry):
            r = pl.ds(pl.multiple_of(i * 32, 32), 32)
            dn = conv[r, :].astype(BF).astype(F32)
            hat = xhat[j, r, :]
            dh = dn * gain[...]
            m1 = jnp.mean(dh, axis=-1, keepdims=True)
            m2 = jnp.mean(dh * hat, axis=-1, keepdims=True)
            d = rstd[j, r, :] * (dh - m1 - hat * m2)
            dc[j, pl.ds(i * 2, 2)] = d.reshape(2, W, D)
            a, b, c = carry
            fold = lambda v: jnp.sum(v.reshape(4, 8, D), axis=0)
            return a + fold(dn * hat), b + fold(dn), c + fold(d)

        zero = jnp.zeros((8, D), F32)
        a, b, c = lax.fori_loop(0, R // 32, norm_rows, (zero, zero, zero))
        ggain[...] += jnp.sum(a, axis=0, keepdims=True)
        gnb[...] += jnp.sum(b, axis=0, keepdims=True)
        gkb[...] += jnp.sum(c, axis=0, keepdims=True)

        @pl.when(s > 0)
        def _():
            col = lax.broadcasted_iota(jnp.int32, (S, W, LANE), 1)

            def back_lanes(c):
                lanes = lanes_of(c)
                fill_shifts(dc[j, :, :, lanes].reshape(R, LANE), shd, lanes)
                total = taps(shd, k, lanes, g[:, :, lanes], True)
                bsend[j, :, :, lanes] = jnp.where(col < S, total, 0.0).astype(BF)

            loop(D // LANE, back_lanes)
            copy.start()

        @pl.when((j == 0) & (s < last))
        def _():
            kernel_grad(0)

    loop(2, bwd)
    lax.fori_loop(jnp.where(s == last, 0, 1), 2, lambda j, c: (kernel_grad(j), c)[1], 0)

    def grad_in(c):
        cols = pl.ds(pl.multiple_of(c * 256, 256), 256)
        new = w1[:, cols] - learning_rate * dot(nrm[...], du[:, cols], 0, 0)
        o_w1[:, cols] = new
        for half in range(2):
            o_tiles[2 * c + half] = new[:, half * TILE : (half + 1) * TILE].astype(BF)

    loop(HID // 256, grad_in)

    def grad_out(r):
        rows = pl.ds(pl.multiple_of(r * D, D), D)
        for c in range(2):
            cols = pl.ds(c * 256, 256)
            new = w2[rows, cols] - learning_rate * dot(h[:, rows], dmb[:, cols], 0, 0)
            o_w2[rows, cols] = new
            for half in range(2):
                o_tiles[16 + (2 * c + half) * 4 + r] = new[:, half * TILE : (half + 1) * TILE].astype(BF)

    loop(HID // D, grad_out)

    for old, grad, new in (
        (k, gk, o_k), (kb, gkb, o_kb), (gain, ggain, o_gain), (nb, gnb, o_nb),
        (b1, gb1, o_b1), (b2, gb2, o_b2), (ls, gls, o_ls),
    ):
        new[...] = old[...] - learning_rate * grad[...]

    for j in range(2):

        @pl.when(s < last)
        def _(j=j):
            to_section(fsend.at[j], frecv.at[j], f_s.at[j], f_r.at[j], up).wait_send()

        @pl.when(s > 0)
        def _(j=j):
            to_section(bsend.at[j], brecv.at[j], b_s.at[j], b_r.at[j], down).wait_send()


def vmem(n):
    return [pl.BlockSpec(memory_space=pltpu.VMEM)] * n


def params(collective, mib=60):
    return pltpu.CompilerParams(
        collective_id=collective, has_side_effects=True, vmem_limit_bytes=mib * 2**20
    )


def train(inputs, cot, small, w1, w2):
    k, kb, gain, nb, b1, b2, ls = small
    row = jax.ShapeDtypeStruct((1, D), F32)
    dma = pltpu.SemaphoreType.DMA
    V = pltpu.VMEM
    wide = (2, S, W, D)
    return pl.pallas_call(
        train_kernel,
        out_shape=(
            jax.ShapeDtypeStruct((7, 7, D), F32), row, row, row,
            jax.ShapeDtypeStruct((D, HID), F32), jax.ShapeDtypeStruct((1, HID), F32),
            jax.ShapeDtypeStruct((HID, D), F32), row, row,
            jax.ShapeDtypeStruct((32, D, TILE), BF),
        ),
        in_specs=vmem(11),
        out_specs=vmem(10),
        scratch_shapes=[
            V((D, HID), BF), V((HID, D), BF), V(wide, F32), V((2, 7, S + 6, W, D), F32),
            V((7, S + 6, W, D), F32), V((R, D), F32), V((2, R, D), F32), V((2, R, 1), F32),
            V((2 * R, D), BF), V((R, HID), F32), V((2 * R, HID), BF), V((2, R, HID), F32),
            V((2, R, D), F32), V((2 * R, D), BF), V((2 * R, HID), BF), V(wide, F32),
            V((S, W, D), F32),
            V((7, 7, D), F32), V((1, D), F32), V((1, D), F32), V((1, D), F32),
            V((1, HID), F32), V((1, D), F32), V((1, D), F32),
            V(wide, BF), V(wide, BF), V(wide, BF), V(wide, BF),
            dma((2,)), dma((2,)), dma((2,)), dma((2,)),
        ],
        compiler_params=params(0),
        name="train",
    )(inputs, cot, k, kb, gain, nb, w1, b1, w2, b2, ls)


def exchange_kernel(block_of, slot_of, marked, tiles, o_w1, o_w2, outgoing, incoming, send, recv):
    me = lax.axis_index("member")
    members = lax.axis_size("member")
    barrier = pltpu.get_barrier_semaphore()

    def greet(t):
        pl.semaphore_signal(
            barrier, inc=1, device_id={"member": lax.rem(me + t, members)}, device_id_type=MESH
        )

    lax.fori_loop(1, members, lambda t, c: (greet(t), c)[1], 0)
    pl.semaphore_wait(barrier, members - 1)

    def copy(t):
        return pltpu.make_async_remote_copy(
            src_ref=outgoing.at[t],
            dst_ref=incoming.at[t],
            send_sem=send.at[t],
            recv_sem=recv.at[t],
            device_id={"member": lax.rem(me + t, members)},
            device_id_type=MESH,
        )

    def push(t):
        outgoing[t] = tiles[block_of[t]]
        copy(t).start()

    lax.fori_loop(1, members, lambda t, c: (push(t), c)[1], 0)
    lax.fori_loop(1, members, lambda t, c: (copy(t).wait_recv(), c)[1], 0)

    def chosen(b):
        return jnp.where(marked[b] == 1, incoming[slot_of[b]], tiles[b])

    def place_in(b):
        o_w1[:, lanes_of(b)] = chosen(b)

    loop(16, place_in)

    def place_out(r):
        for c in range(4):
            o_w2[pl.ds(pl.multiple_of(r * D, D), D), pl.ds(c * TILE, TILE)] = chosen(16 + 4 * c + r)

    loop(4, place_out)
    lax.fori_loop(1, members, lambda t, c: (copy(t).wait_send(), c)[1], 0)


def exchange(tiles, block_of, slot_of, marked):
    smem = pl.BlockSpec(memory_space=pltpu.SMEM)
    dma = pltpu.SemaphoreType.DMA
    return pl.pallas_call(
        exchange_kernel,
        out_shape=(jax.ShapeDtypeStruct((D, HID), BF), jax.ShapeDtypeStruct((HID, D), BF)),
        in_specs=[smem, smem, smem] + vmem(1),
        out_specs=vmem(2),
        scratch_shapes=[
            pltpu.VMEM((32, D, TILE), BF), pltpu.VMEM((32, D, TILE), BF), dma((32,)), dma((32,)),
        ],
        compiler_params=params(1, 24),
        name="exchange",
    )(block_of, slot_of, marked, tiles)


def probe_kernel(
    probe, k, kb, gain, nb, w1, b1, w2, b2, ls,
    out_ref,
    x, sh, conv, nrm, u, h, fsend, frecv, f_s, f_r,
):
    s = lax.axis_index("section")
    last = lax.axis_size("section") - 1
    up = jnp.minimum(s + 1, last)
    neighbours_ready()
    zero_borders(sh)
    copy = to_section(fsend, frecv, f_s, f_r, up)

    @pl.when(s == 0)
    def _():
        x[:, S:W, :] = jnp.zeros((S, W - S, D), F32)
        x[:, 0:S, :] = probe[...].astype(F32)

    @pl.when(s > 0)
    def _():
        copy.wait_recv()
        x[...] = frecv[...].astype(F32)

    def out(values):
        fsend[...] = unpadded(values).astype(BF).reshape(S, W, D)

        @pl.when(s < last)
        def _():
            copy.start()

        out_ref[...] = fsend[:, 0:S, :]

    forward(x, sh, conv, k, kb, gain, nb, w1, b1, w2, b2, ls, u, h, nrm, out, None)

    @pl.when(s < last)
    def _():
        copy.wait_send()


def run_probe(probe, small, w1, w2):
    k, kb, gain, nb, b1, b2, ls = small
    dma = pltpu.SemaphoreType.DMA
    V = pltpu.VMEM
    return pl.pallas_call(
        probe_kernel,
        out_shape=jax.ShapeDtypeStruct((S, S, D), BF),
        in_specs=vmem(10),
        out_specs=vmem(1)[0],
        scratch_shapes=[
            V((S, W, D), F32), V((7, S + 6, W, D), F32), V((R, D), F32), V((R, D), BF),
            V((R, HID), F32), V((R, HID), BF), V((S, W, D), BF), V((S, W, D), BF), dma, dma,
        ],
        compiler_params=params(2, 30),
        name="probe",
    )(probe, k, kb, gain, nb, w1, b1, w2, b2, ls)


def local(
    inputs, cotangent, probe, dw_kernel, dw_bias, norm_gain, norm_bias, w_in, b_in, w_out, b_out,
    layer_scale, shuffle_mask, source_member,
):
    member = lax.axis_index("member")
    members = lax.axis_size("member")
    small = (
        dw_kernel[0, 0], dw_bias[0], norm_gain[0], norm_bias[0], b_in[0], b_out[0], layer_scale[0],
    )
    sources, marked = source_member[0], shuffle_mask[0]
    ids = jnp.arange(32, dtype=jnp.int32)
    block_for = jnp.sum(
        jnp.where((sources == member) & (marked == 1)[:, None], ids[:, None], 0), axis=0
    )
    block_of = jnp.roll(block_for, -member)
    mine = lax.dynamic_index_in_dim(sources, member, axis=1, keepdims=False)
    slot_of = (member - mine + members) % members

    res = train(inputs[0, :, 0], cotangent[0, :, 0], small, w_in[0, 0], w_out[0, 0])
    o_k, o_kb, o_gain, o_nb, u_w1, o_b1, u_w2, o_b2, o_ls, tiles = res
    w1b, w2b = exchange(tiles, block_of, slot_of, marked)
    out = run_probe(probe[0, 0], (o_k, o_kb, o_gain, o_nb, o_b1, o_b2, o_ls), w1b, w2b)

    is_in = jnp.repeat(marked[:16], TILE)[None, :] == 1
    is_out = jnp.repeat(jnp.repeat(marked[16:].reshape(4, 4).T, D, axis=0), TILE, axis=1) == 1
    new_in = jnp.where(is_in, w1b.astype(F32), u_w1)
    new_out = jnp.where(is_out, w2b.astype(F32), u_w2)
    return new_in[None, None], new_out[None, None], out[None, None, None]


def solution(mesh):
    return jax.shard_map(
        local,
        mesh=mesh,
        in_specs=(
            P("member", None, None, None, None, None),
            P("member", None, None, None, None, None),
            P("member", None, None, None, None),
            P("member", "section", None, None, None),
            P("member", "section", None),
            P("member", "section", None),
            P("member", "section", None),
            P("member", "section", None, None),
            P("member", "section", None),
            P("member", "section", None, None),
            P("member", "section", None),
            P("member", "section", None),
            P("section", None),
            P("section", None, None),
        ),
        out_specs=(
            P("member", "section", None, None),
            P("member", "section", None, None),
            P("member", "section", None, None, None, None),
        ),
        check_vma=False,
    )
```

time: 606 us -> 290 us (0.48)
  the two profiles are of different devices: /device:TPU:8 before, /device:TPU:56 now
where the time goes in v1:
time: 290 us
  Pallas kernels  265 us (91%)
  local copies, waits for them, and re-layouts  14.9 us (5%)
  other arithmetic  9.15 us (3%)
    pallas_call x1, Pallas kernels, train(): pl.pallas_call(train_kernel, out_shape=(jax.ShapeDtypeStruct((7, 7, D), F...  101 us
    pallas_call x1, Pallas kernels, run_probe(): pl.pallas_call(probe_kernel, out_shape=jax.ShapeDtypeStruct((S, S, D), BF...  89.1 us
    pallas_call x1, Pallas kernels, exchange(): pl.pallas_call(exchange_kernel, out_shape=(jax.ShapeDtypeStruct((D, HID),...  75.7 us
    broadcast_in_dim x2, other arithmetic, local(): return (new_in[None, None], new_out[None, None], out[None, None, None])  8.69 us
    broadcast_in_dim x1, local copies, waits for them, and re-layouts, local(): jnp.repeat(jnp.repeat(marked[16:].reshape(4, 4).T, D, axis=0), TILE, axis=1)  6.39 us
    unnamed x30, local copies, waits for them, and re-layouts  5.84 us

profile of v1, /device:TPU:56, one launch (start us, length us, event | category | flops | bytes accessed | tf_op | source)
XLA Modules:
  0.0 290.3 jit_solution(3056938612248256209)
XLA Ops:
  0.6 2.2 copy_bitcast_fusion
  2.9 1.6 copy.29
  4.4 0.0 copy-start.6
  4.4 0.0 copy-start.13
  4.4 100.6 %train.1 = (f32[7,7,512]{2,1,0:T(8,128)}, f32[1,512]{1,0:T(1,128)}, f32[1,512]{1,0:T(1,128)}, f32[1,512]{1,0:T(1,128)}, f32[512,2048]{1,0:T(8,128)}, /*index=5*/...) custom-call(bf16[2,14,14,512]{3,2,1,0:T(8,128)(2,1)} %get-tuple-elemen, ...), custom_call_target="tpu_custom_call" | custom-call | tf_op jit(solution)/shard_map/train/pallas_call | solution.py:328
  105.0 0.0 copy-done.6
  105.1 0.0 copy-done.13
  105.1 0.1 select_reduce_fusion
  105.2 0.1 pad_add_fusion
  105.2 0.1 dynamic_slice.8.block_of
  105.3 0.2 add_reduce_fusion
  105.5 0.0 copy-start.2
  105.5 2.2 copy-done.2
  107.7 0.0 copy-start.12
  107.7 75.7 %exchange.1 = (bf16[512,2048]{1,0:T(8,128)(2,1)S(1)}, bf16[2048,512]{1,0:T(8,128)(2,1)S(1)}) custom-call(s32[32]{0:T(128)S(1)} %dynamic_slice.8.block_of, s32[32]{0:T(128)S(1)} %and_select_fusion.slot_of, s32[32]{0:T(128)S(1)} %bitcast.38, bf16[32,512,128]{2,1,0:T(8,128)(2,1)S(1)} %copy-done.2), custom_call_target="tpu_custom_call" | custom-call | tf_op jit(solution)/shard_map/exchange/pallas_call | solution.py:403
  183.4 0.0 copy-start
  183.4 1.4 copy-done
  184.8 0.1 compare_reduce_fusion
  184.9 0.1 broadcast_bitcast_fusion
  184.9 0.0 copy-done.12
  184.9 2.7 select_bitcast_fusion.1
  187.7 0.1 eq.70
  187.7 0.1 copy.22
  187.9 0.1 broadcast_in_dim.45
  187.9 6.4 %broadcast_in_dim.46 = pred[2048,4,128]{2,1,0:T(4,128)(4,1)S(1)} broadcast(pred[2048,4]{1,0:T(8,128)(4,1)S(1)} %bitcast.42), dimensions={0,1} | broadcast | bytes 1056768 | tf_op jit(solution)/shard_map/broadcast_in_dim | solution.py:496
  194.3 0.0 copy-start.1
  194.3 0.0 copy-start.3
  194.4 0.0 copy-start.4
  194.4 0.0 copy-start.5
  194.4 0.0 copy-start.7
  194.4 0.0 copy-start.8
  194.4 0.0 copy-start.9
  194.4 0.0 copy-start.10
  194.4 0.0 copy-start.11
  194.4 6.0 %select_bitcast_fusion = f32[1,1,2048,512]{3,2,1,0:T(8,128)} fusion(f32[2048,512]{1,0:T(8,128)} %get-tuple-element.19, bf16[2048,512]{1,0:T(8,128)(2,1)} %copy-done, pred[256,8,4,128]{3,2,1,0:T(4,128)(4,1)S(1)} %bitcast.41), kind=kLoop, calls=%fused_computation | loop fusion | flops 2097152 | bytes 11534336 | tf_op jit(solution)/shard_map/broadcast_in_dim | solution.py:499
  200.4 0.0 copy-done.1
  200.4 0.0 copy-done.3
  200.4 0.0 copy-done.4
  200.4 0.0 copy-done.5
  200.4 0.0 copy-done.7
  200.4 0.0 copy-done.8
  200.4 0.0 copy-done.9
  200.4 0.0 copy-done.10
  200.5 0.0 copy-done.11
  200.5 89.1 %probe.1 = bf16[14,14,512]{2,1,0:T(8,128)(2,1)S(1)} custom-call(bf16[14,14,512]{2,1,0:T(8,128)(2,1)S(1)} %bitcast.37, f32[7,7,512]{2,1,0:T(8,128)S(1)} %copy-done.4, f32[1,512]{1,0:T(1,128)S(1)} %copy-done.7, f32[1,512]{1,0:T(1,128)S(1)} %copy-done.8, f32[1,512]{1,0:T(1,128)S(1)} %copy-done.9, bf16[512,2048]{1,0:T(8,128)(2,1)S(1)} %get-tuple-element.16.w1, ...), custom_call_target="tpu_custom_call" | custom-call | tf_op jit(solution)/shard_map/probe/pallas_call | solution.py:458
  289.6 0.7 copy.31
  (2 shorter events, 0.0 us)
Async XLA Ops:
  4.4 100.6 %copy-start.6 = (s32[1,32]{1,0:T(1,128)S(1)}, s32[1,32]{1,0:T(1,128)}, u32[]{:S(2)}) copy-start(s32[1,32]{1,0:T(1,128)} %param.26) | copy-start | bytes 388
  4.4 100.6 %copy-start.13 = (s32[1,32,32]{2,1,0:T(8,128)S(1)}, s32[1,32,32]{2,1,0:T(8,128)}, u32[]{:S(2)}) copy-start(s32[1,32,32]{2,1,0:T(8,128)} %param.27) | copy-start | bytes 12292
  105.5 2.2 copy-start.2
  107.7 77.2 %copy-start.12 = (f32[512,2048]{1,0:T(8,128)S(1)}, f32[512,2048]{1,0:T(8,128)}, u32[]{:S(2)}) copy-start(f32[512,2048]{1,0:T(8,128)} %get-tuple-element.17) | copy-start | bytes 12582916
  183.4 1.4 copy-start
  194.3 6.1 %copy-start.1 = (bf16[2048,512]{1,0:T(8,128)(2,1)S(1)}, bf16[2048,512]{1,0:T(8,128)(2,1)}, u32[]{:S(2)}) copy-start(bf16[2048,512]{1,0:T(8,128)(2,1)} %copy-done) | copy-start | bytes 6291460
  194.3 6.1 %copy-start.3 = (bf16[1,1,14,14,512]{4,3,2,1,0:T(8,128)(2,1)S(1)}, bf16[1,1,14,14,512]{4,3,2,1,0:T(8,128)(2,1)}, u32[]{:S(2)}) copy-start(bf16[1,1,14,14,512]{4,3,2,1,0:T(8,128)(2,1)} %param.16) | copy-start | bytes 602116
  194.4 6.0 %copy-start.4 = (f32[7,7,512]{2,1,0:T(8,128)S(1)}, f32[7,7,512]{2,1,0:T(8,128)}, u32[]{:S(2)}) copy-start(f32[7,7,512]{2,1,0:T(8,128)} %get-tuple-element.20.k) | copy-start | bytes 301060
  194.4 6.0 %copy-start.5 = (f32[1,2048]{1,0:T(1,128)S(1)}, f32[1,2048]{1,0:T(1,128)}, u32[]{:S(2)}) copy-start(f32[1,2048]{1,0:T(1,128)} %get-tuple-element.24.b1) | copy-start | bytes 24580
  194.4 6.0 %copy-start.7 = (f32[1,512]{1,0:T(1,128)S(1)}, f32[1,512]{1,0:T(1,128)}, u32[]{:S(2)}) copy-start(f32[1,512]{1,0:T(1,128)} %get-tuple-element.21.kb) | copy-start | bytes 6148
  194.4 6.0 %copy-start.8 = (f32[1,512]{1,0:T(1,128)S(1)}, f32[1,512]{1,0:T(1,128)}, u32[]{:S(2)}) copy-start(f32[1,512]{1,0:T(1,128)} %get-tuple-element.22.gain) | copy-start | bytes 6148
  194.4 6.0 %copy-start.9 = (f32[1,512]{1,0:T(1,128)S(1)}, f32[1,512]{1,0:T(1,128)}, u32[]{:S(2)}) copy-start(f32[1,512]{1,0:T(1,128)} %get-tuple-element.23.nb) | copy-start | bytes 6148
  194.4 6.0 %copy-start.10 = (f32[1,512]{1,0:T(1,128)S(1)}, f32[1,512]{1,0:T(1,128)}, u32[]{:S(2)}) copy-start(f32[1,512]{1,0:T(1,128)} %get-tuple-element.25.b2) | copy-start | bytes 6148
  194.4 6.0 %copy-start.11 = (f32[1,512]{1,0:T(1,128)S(1)}, f32[1,512]{1,0:T(1,128)}, u32[]{:S(2)}) copy-start(f32[1,512]{1,0:T(1,128)} %get-tuple-element.26.ls) | copy-start | bytes 6148

commit v2 on v1

v2 whole, which is shorter than its diff:
```python
import jax
import jax.numpy as jnp
from jax import lax
from jax.experimental import pallas as pl
from jax.experimental.pallas import tpu as pltpu
from jax.sharding import PartitionSpec as P

MESH = pl.DeviceIdType.MESH
BF = jnp.bfloat16
F32 = jnp.float32
S = 14
W = 16
R = S * W
HS, HR = S // 2, R // 2
D = 512
HID = 2048
LANE = 128
TILE = 128
CH = 256
learning_rate = 0.001
norm_epsilon = 1e-06

CHIPS = (
    (0, 0), (0, 1), (1, 0), (0, 3), (3, 0), (1, 1), (3, 3), (1, 3), (3, 1),
    (0, 2), (2, 0), (2, 2), (1, 2), (2, 1), (3, 2), (2, 3),
)
ORDER = tuple(z * 8 + x * 2 + c for c in (1, 0) for z, x in CHIPS if (z, x, c) != (0, 0, 0))


def at_distance(me, t, sign=1):
    z = lax.rem(me // 8 + sign * (t // 8) + 4, 4)
    x = lax.rem(lax.rem(me // 2, 4) + sign * (t // 2 % 4) + 4, 4)
    c = lax.rem(lax.rem(me, 2) + t % 2, 2)
    return z * 8 + x * 2 + c


def dot(a, b, ca, cb):
    return lax.dot_general(a, b, (((ca,), (cb,)), ((), ())), preferred_element_type=F32)


def loop(n, body):
    lax.fori_loop(0, n, lambda i, c: (body(i), c)[1], 0)


def lanes_of(c):
    return pl.ds(pl.multiple_of(c * LANE, LANE), LANE)


def half_rows(half, base=0):
    return pl.ds(pl.multiple_of(base + half * HR, HR), HR)


def conv_half(src, sh, k, total, start, half, flip):
    base = half * HS
    rows = range(0, HS + 3) if half == 0 else range(HS - 3, S)
    begun = () if half == 0 else range(HS - 3, HS + 3)

    def per_lanes(c):
        lanes = lanes_of(c)
        v = src[base : base + HS, :, lanes]
        col = lax.broadcasted_iota(jnp.int32, (HS, W, LANE), 1)
        for dj in range(7):
            d = dj - 3
            moved = v if d == 0 else pltpu.roll(v, (-d) % W, 1)
            sh[dj, base : base + HS, :, lanes] = jnp.where((col + d >= 0) & (col + d < S), moved, 0.0)
        acc = {r: total[r, :, lanes] if r in begun else start(r, lanes) for r in rows}
        for dj in range(7):
            ks = [k[6 - di, 6 - dj, :, lanes] if flip else k[di, dj, :, lanes] for di in range(7)]
            for i in range(base, base + HS):
                x = sh[dj, i, :, lanes]
                for r in rows:
                    if abs(r - i) <= 3:
                        acc[r] = acc[r] + ks[i - r + 3] * x
        for r in rows:
            total[r, :, lanes] = acc[r]

    loop(D // LANE, per_lanes)


def gelu_parts(x):
    t = 1.0 / (1.0 + 0.23164189 * jnp.abs(x))
    e = jnp.exp(-0.5 * (x * x))
    poly = t * (
        0.127414796
        + t * (-0.142248368 + t * (0.7107068705 + t * (-0.7265760135 + t * 0.5307027145)))
    )
    q = poly * e
    return jnp.where(x < 0.0, q, 1.0 - q), e


def forward(take, x, sh, conv, k, kb, gain, nb, w1, b1, w2, b2, ls, h, n, give, before, keep):
    def bias(r, lanes):
        return jnp.broadcast_to(kb[:, lanes], (W, LANE))

    for half in range(2):
        take(half)
        conv_half(x, sh, k, conv, bias, half, False)
    before()
    for half in range(2):
        rows = slice(half * HR, half * HR + HR)
        c = conv[half * HS : half * HS + HS].reshape(HR, D)
        off = c - jnp.mean(c, axis=-1, keepdims=True)
        var = jnp.mean(off * off, axis=-1, keepdims=True)
        rstd = lax.rsqrt(var + norm_epsilon)
        hat = off * rstd
        n[rows, :] = (hat * gain[...] + nb[...]).astype(BF)
        if keep is not None:
            keep[0][rows, :] = hat
            keep[1][rows, :] = rstd
        for c in range(HID // CH):
            cols = slice(c * CH, c * CH + CH)
            a = dot(n[rows, :], w1[:, cols], 1, 0) + b1[:, cols]
            phi, e = gelu_parts(a)
            h[rows, cols] = (a * phi).astype(BF)
            if keep is not None:
                keep[2][rows, cols] = phi + a * e * 0.3989422804014327
        mixed = dot(h[rows, :], w2[...], 1, 0) + b2[...]
        if keep is not None:
            keep[3][rows, :] = mixed
        give(half, x[half * HS : half * HS + HS].reshape(HR, D) + ls[...] * mixed)


def unpadded(values):
    col = lax.broadcasted_iota(jnp.int32, values.shape, 1)
    return jnp.where(col < S, values, 0.0)


def to_section(src, dst, send, recv, section):
    return pltpu.make_async_remote_copy(
        src_ref=src,
        dst_ref=dst,
        send_sem=send,
        recv_sem=recv,
        device_id={"section": section},
        device_id_type=MESH,
    )


def greet_sections(barrier):
    s = lax.axis_index("section")
    count = lax.axis_size("section")
    for other in (lax.rem(s + 1, count), lax.rem(s + count - 1, count)):
        pl.semaphore_signal(barrier, inc=1, device_id={"section": other}, device_id_type=MESH)


def train_kernel(
    sources, marked,
    inputs, cot, k, kb, gain, nb, w1, b1, w2, b2, ls,
    o_w1, o_w2, o_s1, o_s2, o_k, o_kb, o_gain, o_nb, o_b1, o_b2, o_ls,
    w1f, w2f, w1b, w2b, x, sh, shd, conv, xhat, rstd, nrm, h, gp, mixed, dmb, du, dc, g,
    pt, gkb, ggain, gnb, gb1, gb2, gls, tiles, outgoing, incoming,
    fsend, frecv, bsend, brecv, f_s, f_r, b_s, b_r, w_in, w_out, e_s, e_r, block_of,
):
    s = lax.axis_index("section")
    last = lax.axis_size("section") - 1
    up = jnp.minimum(s + 1, last)
    down = jnp.maximum(s - 1, 0)
    me = lax.axis_index("member")

    loads = [
        pltpu.make_async_copy(w1, w1f, w_in.at[0]),
        pltpu.make_async_copy(w2, w2f, w_in.at[1]),
    ]
    for load in loads:
        load.start()
    barrier = pltpu.get_barrier_semaphore()
    greet_sections(barrier)
    for t in ORDER:
        pl.semaphore_signal(
            barrier, inc=1, device_id={"member": at_distance(me, t)}, device_id_type=MESH
        )
    for ref in (pt, gkb, ggain, gnb, gb1, gb2, gls):
        ref[...] = jnp.zeros_like(ref)
    pl.semaphore_wait(barrier, 2 + len(ORDER))

    def tables():
        def per_slot(t):
            to = at_distance(me, t)
            block = jnp.int32(0)
            for b in range(32):
                block = jnp.where((sources[b, to] == me) & (marked[b] == 1), b, block)
            block_of[t] = block

        loop(32, per_slot)

    @pl.when(s > 0)
    def _():
        tables()

    def take(half, first, given, arrived, wait, dst):
        rows = slice(half * HS, half * HS + HS)

        @pl.when(first)
        def _():
            dst[rows, S:W, :] = jnp.zeros((HS, W - S, D), F32)
            dst[rows, 0:S, :] = given[rows].astype(F32)

        @pl.when(jnp.logical_not(first))
        def _():
            wait()
            dst[rows] = arrived[rows].astype(F32)

    def half_copy(send, recv, sems, j, half, section):
        rows = pl.ds(half * HS, HS)
        return to_section(
            send.at[j, rows], recv.at[j, rows], sems[0].at[j, half], sems[1].at[j, half], section
        )

    def fwd_copy(j, half):
        return half_copy(fsend, frecv, (f_s, f_r), j, half, up)

    def bwd_copy(j, half):
        return half_copy(bsend, brecv, (b_s, b_r), j, half, down)

    def fwd(j):
        rows = pl.ds(pl.multiple_of(j * R, R), R)

        def before():
            @pl.when(j == 0)
            def _():
                for load in loads:
                    load.wait()

                def cast(i):
                    r = pl.ds(pl.multiple_of(i * 32, 32), 32)
                    w1b[r, :] = w1f[r, :].astype(BF)
                    r = pl.ds(pl.multiple_of(i * 128, 128), 128)
                    w2b[r, :] = w2f[r, :].astype(BF)

                loop(16, cast)

        def give(half, values):
            @pl.when(s < last)
            def _():
                fsend[j, half * HS : half * HS + HS] = unpadded(values.reshape(HS, W, D)).astype(BF)
                fwd_copy(j, half).start()

        forward(
            lambda half: take(
                half, s == 0, inputs.at[j], frecv.at[j], fwd_copy(j, half).wait_recv, x.at[j]
            ),
            x.at[j], sh.at[j], conv, k, kb, gain, nb, w1b, b1, w2b, b2, ls,
            h.at[rows, :], nrm.at[rows, :], give, before,
            (xhat.at[j], rstd.at[j], gp.at[j], mixed.at[j]),
        )

    loop(2, fwd)

    @pl.when(s == 0)
    def _():
        tables()

    def kernel_grad(j):
        def per_lanes(c):
            lanes = lanes_of(c)
            for dj in range(7):
                acc = [None] * 7
                for r in range(S):
                    d = dc[j, r, :, lanes]
                    for di in range(7):
                        if 0 <= r + di - 3 < S:
                            p = d * sh[j, dj, r + di - 3, :, lanes]
                            acc[di] = p if acc[di] is None else acc[di] + p
                for di in range(7):
                    pt[di, dj, :, lanes] += acc[di][0:8] + acc[di][8:16]

        loop(D // LANE, per_lanes)

    def bwd(j):
        def nothing(r, lanes):
            return jnp.zeros((W, LANE), F32)

        for half in range(2):
            base = pl.multiple_of(j * R, R)
            rows = slice(half * HR, half * HR + HR)
            both = half_rows(half, base)
            take(half, s == last, cot.at[j], brecv.at[j], bwd_copy(j, half).wait_recv, g)
            flat = g[half * HS : half * HS + HS].reshape(HR, D)
            dm = flat * ls[...]
            dmb[both, :] = dm.astype(BF)
            gb2[...] += jnp.sum(dm, axis=0, keepdims=True)
            gls[...] += jnp.sum(flat * mixed[j, rows, :], axis=0, keepdims=True)
            for c in range(HID // CH):
                cols = slice(c * CH, c * CH + CH)
                a = dot(dmb[both, :], w2b[cols, :], 1, 1) * gp[j, rows, cols]
                du[both, cols] = a.astype(BF)
                gb1[:, cols] += jnp.sum(a, axis=0, keepdims=True)
            dn = dot(du[both, :], w1b[...], 1, 1)
            hat = xhat[j, rows, :]
            dh = dn * gain[...]
            m1 = jnp.mean(dh, axis=-1, keepdims=True)
            m2 = jnp.mean(dh * hat, axis=-1, keepdims=True)
            d = rstd[j, rows, :] * (dh - m1 - hat * m2)
            dc[j, half * HS : half * HS + HS] = d.reshape(HS, W, D)
            ggain[...] += jnp.sum(dn * hat, axis=0, keepdims=True)
            gnb[...] += jnp.sum(dn, axis=0, keepdims=True)
            gkb[...] += jnp.sum(d, axis=0, keepdims=True)

            @pl.when(s > 0)
            def _(half=half):
                conv_half(dc.at[j], shd, k, conv, nothing, half, True)

        @pl.when(s > 0)
        def _():
            for half in range(2):
                part = slice(half * HS, half * HS + HS)
                bsend[j, part] = unpadded(g[part] + conv[part]).astype(BF)
                bwd_copy(j, half).start()

        @pl.when((j == 0) & (s < last))
        def _():
            kernel_grad(0)

    loop(2, bwd)

    stores = []

    def store(src, dst):
        copy = pltpu.make_async_copy(src, dst, w_out.at[len(stores)])
        copy.start()
        stores.append(copy)

    for c in range(4):
        cols = pl.ds(c * 512, 512)
        new = w1f[:, cols] - learning_rate * dot(nrm[...], du[:, cols], 0, 0)
        w1f[:, cols] = new
        for q in range(4):
            tiles[4 * c + q] = new[:, q * TILE : (q + 1) * TILE].astype(BF)
    for r in range(HID // D):
        rows = pl.ds(r * D, D)
        new = w2f[rows, :] - learning_rate * dot(h[:, rows], dmb[...], 0, 0)
        w2f[rows, :] = new
        for q in range(4):
            tiles[16 + 4 * q + r] = new[:, q * TILE : (q + 1) * TILE].astype(BF)

    def push_copy(t):
        return pltpu.make_async_remote_copy(
            src_ref=outgoing.at[t],
            dst_ref=incoming.at[t],
            send_sem=e_s.at[t],
            recv_sem=e_r.at[t],
            device_id={"member": at_distance(me, t)},
            device_id_type=MESH,
        )

    for t in ORDER:
        outgoing[t] = tiles[block_of[t]]
        push_copy(t).start()

    store(w1f, o_w1)
    store(w2f, o_w2)
    lax.fori_loop(jnp.where(s == last, 0, 1), 2, lambda j, c: (kernel_grad(j), c)[1], 0)
    for di in range(7):
        for dj in range(7):
            o_k[di, dj] = k[di, dj] - learning_rate * jnp.sum(pt[di, dj], axis=0, keepdims=True)
    for old, grad, new in (
        (kb, gkb, o_kb), (gain, ggain, o_gain), (nb, gnb, o_nb),
        (b1, gb1, o_b1), (b2, gb2, o_b2), (ls, gls, o_ls),
    ):
        new[...] = old[...] - learning_rate * grad[...]

    for t in ORDER:
        push_copy(t).wait_recv()

    def chosen(b):
        source = sources[b, me]
        z = lax.rem(me // 8 - source // 8 + 4, 4)
        x = lax.rem(lax.rem(me // 2, 4) - lax.rem(source // 2, 4) + 4, 4)
        c = lax.rem(lax.rem(me, 2) + lax.rem(source, 2), 2)
        return jnp.where(marked[b] == 1, incoming[z * 8 + x * 2 + c], tiles[b])

    def place_in(b):
        w1b[:, lanes_of(b)] = chosen(b)

    loop(16, place_in)
    store(w1b, o_s1)

    def place_out(r):
        for c in range(4):
            w2b[pl.ds(pl.multiple_of(r * D, D), D), pl.ds(c * TILE, TILE)] = chosen(16 + 4 * c + r)

    loop(4, place_out)
    store(w2b, o_s2)

    for copy in stores:
        copy.wait()
    for t in ORDER:
        push_copy(t).wait_send()
    for j in range(2):
        for half in range(2):

            @pl.when(s < last)
            def _(j=j, half=half):
                fwd_copy(j, half).wait_send()

            @pl.when(s > 0)
            def _(j=j, half=half):
                bwd_copy(j, half).wait_send()


def vmem(n):
    return [pl.BlockSpec(memory_space=pltpu.VMEM)] * n


def hbm(n):
    return [pl.BlockSpec(memory_space=pltpu.HBM)] * n


def params(collective, mib):
    return pltpu.CompilerParams(
        collective_id=collective, has_side_effects=True, vmem_limit_bytes=mib * 2**20
    )


def train(tables, inputs, cot, small, w1, w2):
    k, kb, gain, nb, b1, b2, ls = small
    dma = pltpu.SemaphoreType.DMA
    V = pltpu.VMEM
    shape = jax.ShapeDtypeStruct
    row = shape((1, D), F32)
    wide = (2, S, W, D)
    return pl.pallas_call(
        train_kernel,
        out_shape=(
            shape((D, HID), F32), shape((HID, D), F32), shape((D, HID), BF), shape((HID, D), BF),
            shape((7, 7, 1, D), F32), row, row, row, shape((1, HID), F32), row, row,
        ),
        in_specs=[pl.BlockSpec(memory_space=pltpu.SMEM)] * 2 + vmem(6) + hbm(1) + vmem(1) + hbm(1) + vmem(2),
        out_specs=hbm(4) + vmem(7),
        scratch_shapes=[
            V((D, HID), F32), V((HID, D), F32), V((D, HID), BF), V((HID, D), BF),
            V(wide, F32), V((2, 7, S, W, D), F32), V((7, S, W, D), F32), V((S, W, D), F32),
            V((2, R, D), F32), V((2, R, 1), F32), V((2 * R, D), BF), V((2 * R, HID), BF),
            V((2, R, HID), F32), V((2, R, D), F32), V((2 * R, D), BF), V((2 * R, HID), BF),
            V(wide, F32), V((S, W, D), F32),
            V((7, 7, 8, D), F32), V((1, D), F32), V((1, D), F32), V((1, D), F32),
            V((1, HID), F32), V((1, D), F32), V((1, D), F32),
            V((32, D, TILE), BF), V((32, D, TILE), BF), V((32, D, TILE), BF),
            V(wide, BF), V(wide, BF), V(wide, BF), V(wide, BF),
            dma((2, 2)), dma((2, 2)), dma((2, 2)), dma((2, 2)), dma((2,)), dma((4,)),
            dma((32,)), dma((32,)), pltpu.SMEM((32,), jnp.int32),
        ],
        compiler_params=params(0, 60),
        name="train",
    )(*tables, inputs, cot, k, kb, gain, nb, w1, b1, w2, b2, ls)


def probe_kernel(
    probe, k, kb, gain, nb, w1_hbm, b1, w2_hbm, b2, ls, after,
    out_ref,
    w1, w2, x, sh, conv, nrm, h, fsend, frecv, f_s, f_r, w_in,
):
    s = lax.axis_index("section")
    last = lax.axis_size("section") - 1
    up = jnp.minimum(s + 1, last)
    loads = [
        pltpu.make_async_copy(w1_hbm, w1, w_in.at[0]),
        pltpu.make_async_copy(w2_hbm, w2, w_in.at[1]),
    ]
    for load in loads:
        load.start()
    barrier = pltpu.get_barrier_semaphore()
    greet_sections(barrier)
    pl.semaphore_wait(barrier, 2)

    def loaded():
        for load in loads:
            load.wait()

    def copy(half):
        rows = pl.ds(half * HS, HS)
        return to_section(fsend.at[rows], frecv.at[rows], f_s.at[half], f_r.at[half], up)

    def take(half):
        rows = slice(half * HS, half * HS + HS)

        @pl.when(s == 0)
        def _():
            x[rows, S:W, :] = jnp.zeros((HS, W - S, D), F32)
            x[rows, 0:S, :] = probe[rows].astype(F32)

        @pl.when(s > 0)
        def _():
            copy(half).wait_recv()
            x[rows] = frecv[rows].astype(F32)

    def give(half, values):
        rows = slice(half * HS, half * HS + HS)
        fsend[rows] = unpadded(values.reshape(HS, W, D)).astype(BF)

        @pl.when(s < last)
        def _():
            copy(half).start()

        out_ref[rows] = fsend[rows, 0:S, :]

    forward(
        take, x, sh, conv, k, kb, gain, nb, w1, b1, w2, b2, ls, h, nrm, give, loaded, None
    )

    @pl.when(s < last)
    def _():
        for half in range(2):
            copy(half).wait_send()


def run_probe(probe, small, w1, w2, after):
    k, kb, gain, nb, b1, b2, ls = small
    dma = pltpu.SemaphoreType.DMA
    V = pltpu.VMEM
    return pl.pallas_call(
        probe_kernel,
        out_shape=jax.ShapeDtypeStruct((S, S, D), BF),
        in_specs=vmem(5) + hbm(1) + vmem(1) + hbm(1) + vmem(2) + hbm(1),
        out_specs=vmem(1)[0],
        scratch_shapes=[
            V((D, HID), BF), V((HID, D), BF), V((S, W, D), F32), V((7, S, W, D), F32), V((S, W, D), F32), V((R, D), BF),
            V((R, HID), BF), V((S, W, D), BF), V((S, W, D), BF), dma((2,)), dma((2,)), dma((2,)),
        ],
        compiler_params=params(1, 24),
        name="probe",
    )(probe, k, kb, gain, nb, w1, b1, w2, b2, ls, after)


PARTS = 8


def finish_kernel(first, *refs):
    if first:
        marked, u1, u2, s1, s2, o1, o2, f1, f2, b1, b2, sem, out = refs
    else:
        marked, u1, u2, s1, s2, _, _, _, o1, o2, f1, f2, b1, b2, sem, out = refs
    s = lax.axis_index("section")

    @pl.when(s > 0 if first else s == 0)
    def _():
        def rows_of(i):
            return pl.ds(i * (D // PARTS), D // PARTS), pl.ds(i * (HID // PARTS), HID // PARTS)

        ins, outs = [], []
        for i in range(PARTS):
            r1, r2 = rows_of(i)
            pairs = ((u1, f1, r1), (u2, f2, r2), (s1, b1, r1), (s2, b2, r2))
            ins.append(
                [
                    pltpu.make_async_copy(a.at[r, :], b.at[r, :], sem.at[i, q])
                    for q, (a, b, r) in enumerate(pairs)
                ]
            )
            outs.append(
                [
                    pltpu.make_async_copy(a.at[r, :], b.at[r, :], out.at[i, q])
                    for q, (a, b, r) in enumerate(((f1, o1, r1), (f2, o2, r2)))
                ]
            )
        for part in ins:
            for copy in part:
                copy.start()
        for i in range(PARTS):
            r1, r2 = rows_of(i)
            for copy in ins[i]:
                copy.wait()
            for c in range(16):
                at = (r1, pl.ds(c * TILE, TILE))
                f1[at] = jnp.where(marked[c] == 1, b1[at].astype(F32), f1[at])
            outs[i][0].start()
            for c in range(4):
                at = (r2, pl.ds(c * TILE, TILE))
                b = 16 + 4 * c + i // (PARTS // 4)
                f2[at] = jnp.where(marked[b] == 1, b2[at].astype(F32), f2[at])
            outs[i][1].start()
        for part in outs:
            for copy in part:
                copy.wait()


def finish(marked, weights, earlier):
    dma = pltpu.SemaphoreType.DMA
    V = pltpu.VMEM
    first = not earlier
    return pl.pallas_call(
        lambda *refs: finish_kernel(first, *refs),
        out_shape=(jax.ShapeDtypeStruct((D, HID), F32), jax.ShapeDtypeStruct((HID, D), F32)),
        in_specs=[pl.BlockSpec(memory_space=pltpu.SMEM)] + hbm(4 + len(earlier)),
        out_specs=hbm(2),
        scratch_shapes=[
            V((D, HID), F32), V((HID, D), F32), V((D, HID), BF), V((HID, D), BF),
            dma((PARTS, 4)), dma((PARTS, 2)),
        ],
        input_output_aliases={} if first else {5: 0, 6: 1},
        compiler_params=pltpu.CompilerParams(vmem_limit_bytes=24 * 2**20),
        name="finish" if first else "finish_zero",
    )(marked, *weights, *earlier)


def local(
    inputs, cotangent, probe, dw_kernel, dw_bias, norm_gain, norm_bias, w_in, b_in, w_out, b_out,
    layer_scale, shuffle_mask, source_member,
):
    small = (
        dw_kernel[0, 0][:, :, None, :], dw_bias[0], norm_gain[0], norm_bias[0], b_in[0], b_out[0],
        layer_scale[0],
    )
    marked = shuffle_mask[0]
    res = train(
        (source_member[0], marked), inputs[0, :, 0], cotangent[0, :, 0], small, w_in[0, 0], w_out[0, 0]
    )
    weights, fresh = res[:4], res[4:]
    earlier = finish(marked, weights, ())
    out = run_probe(probe[0, 0], fresh, weights[2], weights[3], earlier[0])
    new_in, new_out = finish(marked, weights, (*earlier, out))
    return new_in[None, None], new_out[None, None], out[None, None, None]


def solution(mesh):
    return jax.shard_map(
        local,
        mesh=mesh,
        in_specs=(
            P("member", None, None, None, None, None),
            P("member", None, None, None, None, None),
            P("member", None, None, None, None),
            P("member", "section", None, None, None),
            P("member", "section", None),
            P("member", "section", None),
            P("member", "section", None),
            P("member", "section", None, None),
            P("member", "section", None),
            P("member", "section", None, None),
            P("member", "section", None),
            P("member", "section", None),
            P("section", None),
            P("section", None, None),
        ),
        out_specs=(
            P("member", "section", None, None),
            P("member", "section", None, None),
            P("member", "section", None, None, None, None),
        ),
        check_vma=False,
    )
```

time: 290 us -> 179 us (0.62)
  Pallas kernels: 265 us -> 164 us
  other arithmetic: 9.15 us -> 0 us
    pallas_call x2 -> x3, Pallas kernels: 176 us -> 115 us  [the longest x1 109 us: train(): pl.pallas_call(train_kernel, out_shape=(shape((D, HID), F32), shape((HID,...]
    pallas_call x1, Pallas kernels: 89.1 us -> 49.1 us  [run_probe(): pl.pallas_call(probe_kernel, out_shape=jax.ShapeDtypeStruct((S, S, D), BF...]
    broadcast_in_dim x2 -> x0, other arithmetic: 8.69 us -> none  [local(): return (new_in[None, None], new_out[None, None], out[None, None, None])]
    broadcast_in_dim x2 -> x0, local copies, waits for them, and re-layouts: 6.47 us -> none  [the longest x1 6.39 us: local(): jnp.repeat(jnp.repeat(marked[16:].reshape(4, 4).T, D, axis=0), TILE, axis=1)]
    unnamed x30 -> x35, local copies, waits for them, and re-layouts: 5.84 us -> 10.5 us
where the time goes in v2:
time: 179 us; the launch traced here: 178 us
  Pallas kernels  164 us (92%)
  local copies, waits for them, and re-layouts  12.7 us (7%)
    pallas_call x1, Pallas kernels, train(): pl.pallas_call(train_kernel, out_shape=(shape((D, HID), F32), shape((HID,...  109 us
    pallas_call x1, Pallas kernels, run_probe(): pl.pallas_call(probe_kernel, out_shape=jax.ShapeDtypeStruct((S, S, D), BF...  49.1 us
    unnamed x35, local copies, waits for them, and re-layouts  10.5 us
    pallas_call x2, Pallas kernels, finish(): pl.pallas_call(lambda *refs: finish_kernel(first, *refs), out_shape=(jax....  6.34 us

profile of v2, /device:TPU:56, one launch (start us, length us, event | category | flops | bytes accessed | tf_op | source)
XLA Modules:
  0.0 177.8 jit_solution(10483327302323450535)
XLA Ops:
  0.6 2.2 %copy_bitcast_fusion = (bf16[2,14,14,512]{3,2,1,0:T(8,128)(2,1)}, bf16[2,14,14,512]{3,2,1,0:T(8,128)(2,1)}) fusion(bf16[1,2,1,14,14,512]{5,1,4,3,2,0:T(2,128)(2,1)} %param.15, bf16[1,2,1,14,14,512]{5,1,4,3,2,0:T(2,128)(2,1)} %param.14), kind=kLoop, calls=%fused_computation | loop fusion | bytes 1605632 | tf_op jit(solution)/shard_map/squeeze | solution.py:606
  2.9 0.0 copy-start.11
  2.9 108.9 %train.1 = (f32[512,2048]{1,0:T(8,128)}, f32[2048,512]{1,0:T(8,128)}, bf16[512,2048]{1,0:T(8,128)(2,1)}, bf16[2048,512]{1,0:T(8,128)(2,1)}, f32[7,7,1,512]{3,2,1...) custom-call(s32[32,32]{1,0:T(8,128)} %bitcast.29, ...), custom_call_target="tpu_custom_call" | custom-call | tf_op jit(solution)/shard_map/train/pallas_call | solution.py:422
  111.8 0.0 copy-done.11
  111.8 0.0 copy-start
  111.8 1.6 copy-done
  113.4 0.0 copy-start.2
  113.4 1.6 copy-done.2
  114.9 0.0 copy-start.3
  114.9 2.2 %copy-done.3 = f32[512,2048]{1,0:T(8,128)S(1)} copy-done((f32[512,2048]{1,0:T(8,128)S(1)}, f32[512,2048]{1,0:T(8,128)}, u32[]{:S(2)}) %copy-start.3) | copy-done | bytes 4194328
  117.1 0.0 copy-start.5
  117.1 2.2 %copy-done.5 = f32[2048,512]{1,0:T(8,128)S(1)} copy-done((f32[2048,512]{1,0:T(8,128)S(1)}, f32[2048,512]{1,0:T(8,128)}, u32[]{:S(2)}) %copy-start.5) | copy-done | bytes 4194328
  119.3 0.0 copy-start.1
  119.3 0.0 copy-start.8
  119.3 0.0 copy-start.9
  119.3 0.0 copy-start.10
  119.3 0.0 copy-start.12
  119.3 0.0 copy-start.13
  119.4 0.0 copy-start.14
  119.4 0.0 copy-start.15
  119.4 0.0 copy-start.16
  119.4 5.4 %finish.1 = (f32[512,2048]{1,0:T(8,128)}, f32[2048,512]{1,0:T(8,128)}) custom-call(s32[32]{0:T(128)S(1)} %bitcast.23, f32[512,2048]{1,0:T(8,128)S(1)} %copy-done.3, f32[2048,512]{1,0:T(8,128)S(1)} %copy-done.5, bf16[512,2048]{1,0:T(8,128)(2,1)S(1)} %copy-done, bf16[2048,512]{1,0:T(8,128)(2,1)S(1)} %copy-done.2), custom_call_target="tpu_custom_call" | custom-call | tf_op jit(solution)/shard_map/finish/pallas_call | solution.py:581
  124.7 0.0 copy-done.1
  124.8 0.0 copy-done.8
  124.8 0.0 copy-done.9
  124.8 0.0 copy-done.10
  124.8 0.0 copy-done.12
  124.8 0.0 copy-done.13
  124.8 0.0 copy-done.14
  124.8 0.0 copy-done.15
  124.8 0.0 copy-done.16
  124.8 0.0 copy-start.7
  124.8 2.2 %copy-done.7 = f32[512,2048]{1,0:T(8,128)S(1)} copy-done((f32[512,2048]{1,0:T(8,128)S(1)}, f32[512,2048]{1,0:T(8,128)}, u32[]{:S(2)}) %copy-start.7) | copy-done | bytes 4194328
  127.0 0.0 copy-start.4
  127.0 0.0 copy-start.6
  127.0 49.1 %probe.1.refs_7_ = bf16[14,14,512]{2,1,0:T(8,128)(2,1)S(1)} custom-call(bf16[14,14,512]{2,1,0:T(8,128)(2,1)S(1)} %bitcast.21, f32[7,7,1,512]{3,2,1,0:T(1,128)S(1)} %copy-done.9, f32[1,512]{1,0:T(1,128)S(1)} %copy-done.12, f32[1,512]{1,0:T(1,128)S(1)} %copy-done.13, f32[1,512]{1,0:T(1,128)S(1)} %copy-done.14, bf16[512,2048]{1,0:T(8,128)(2,1)S(1)} %copy-done.1, ...), custom_call_target="tpu_custom_call" | custom-call | tf_op jit(solution)/shard_map/probe/pallas_call | solution.py:511
  176.1 0.0 copy-done.4
  176.1 0.0 copy-done.6
  176.1 1.0 finish_zero.1
  177.1 0.7 copy.26
Async XLA Ops:
  2.9 108.9 %copy-start.11 = (s32[1,32]{1,0:T(1,128)S(1)}, s32[1,32]{1,0:T(1,128)}, u32[]{:S(2)}) copy-start(s32[1,32]{1,0:T(1,128)} %param.26) | copy-start | bytes 388
  111.8 1.6 copy-start
  113.4 1.6 copy-start.2
  114.9 2.2 %copy-start.3 = (f32[512,2048]{1,0:T(8,128)S(1)}, f32[512,2048]{1,0:T(8,128)}, u32[]{:S(2)}) copy-start(f32[512,2048]{1,0:T(8,128)} %get-tuple-element.18.refs_1_) | copy-start | bytes 12582916
  117.1 2.2 %copy-start.5 = (f32[2048,512]{1,0:T(8,128)S(1)}, f32[2048,512]{1,0:T(8,128)}, u32[]{:S(2)}) copy-start(f32[2048,512]{1,0:T(8,128)} %get-tuple-element.19.refs_2_) | copy-start | bytes 12582916
  119.3 5.4 %copy-start.1 = (bf16[512,2048]{1,0:T(8,128)(2,1)S(1)}, bf16[512,2048]{1,0:T(8,128)(2,1)}, u32[]{:S(2)}) copy-start(bf16[512,2048]{1,0:T(8,128)(2,1)} %get-tuple-element.20.refs_3_.w1_hbm) | copy-start | bytes 6291460
  119.3 5.4 %copy-start.8 = (bf16[1,1,14,14,512]{4,3,2,1,0:T(8,128)(2,1)S(1)}, bf16[1,1,14,14,512]{4,3,2,1,0:T(8,128)(2,1)}, u32[]{:S(2)}) copy-start(bf16[1,1,14,14,512]{4,3,2,1,0:T(8,128)(2,1)} %param.16) | copy-start | bytes 602116
  119.3 5.4 %copy-start.9 = (f32[7,7,1,512]{3,2,1,0:T(1,128)S(1)}, f32[7,7,1,512]{3,2,1,0:T(1,128)}, u32[]{:S(2)}) copy-start(f32[7,7,1,512]{3,2,1,0:T(1,128)} %get-tuple-element.24.k) | copy-start | bytes 301060
  119.3 5.4 %copy-start.10 = (f32[1,2048]{1,0:T(1,128)S(1)}, f32[1,2048]{1,0:T(1,128)}, u32[]{:S(2)}) copy-start(f32[1,2048]{1,0:T(1,128)} %get-tuple-element.28.b1) | copy-start | bytes 24580
  119.3 5.5 %copy-start.12 = (f32[1,512]{1,0:T(1,128)S(1)}, f32[1,512]{1,0:T(1,128)}, u32[]{:S(2)}) copy-start(f32[1,512]{1,0:T(1,128)} %get-tuple-element.25.kb) | copy-start | bytes 6148
  119.3 5.5 %copy-start.13 = (f32[1,512]{1,0:T(1,128)S(1)}, f32[1,512]{1,0:T(1,128)}, u32[]{:S(2)}) copy-start(f32[1,512]{1,0:T(1,128)} %get-tuple-element.26.gain) | copy-start | bytes 6148
  119.4 5.5 %copy-start.14 = (f32[1,512]{1,0:T(1,128)S(1)}, f32[1,512]{1,0:T(1,128)}, u32[]{:S(2)}) copy-start(f32[1,512]{1,0:T(1,128)} %get-tuple-element.27.nb) | copy-start | bytes 6148
  119.4 5.5 %copy-start.15 = (f32[1,512]{1,0:T(1,128)S(1)}, f32[1,512]{1,0:T(1,128)}, u32[]{:S(2)}) copy-start(f32[1,512]{1,0:T(1,128)} %get-tuple-element.29.b2) | copy-start | bytes 6148
  119.4 5.5 %copy-start.16 = (f32[1,512]{1,0:T(1,128)S(1)}, f32[1,512]{1,0:T(1,128)}, u32[]{:S(2)}) copy-start(f32[1,512]{1,0:T(1,128)} %get-tuple-element.30.ls) | copy-start | bytes 6148
  124.8 2.2 %copy-start.7 = (f32[512,2048]{1,0:T(8,128)S(1)}, f32[512,2048]{1,0:T(8,128)}, u32[]{:S(2)}) copy-start(f32[512,2048]{1,0:T(8,128)} %get-tuple-element.22.after.refs_5_) | copy-start | bytes 12582916
  127.0 49.1 %copy-start.4 = (f32[512,2048]{1,0:T(8,128)S(1)}, f32[512,2048]{1,0:T(8,128)}, u32[]{:S(2)}) copy-start(f32[512,2048]{1,0:T(8,128)} %get-tuple-element.18.refs_1_) | copy-start | bytes 12582916
  127.0 49.1 %copy-start.6 = (f32[2048,512]{1,0:T(8,128)S(1)}, f32[2048,512]{1,0:T(8,128)}, u32[]{:S(2)}) copy-start(f32[2048,512]{1,0:T(8,128)} %get-tuple-element.19.refs_2_) | copy-start | bytes 12582916

commit v3 on v2

--- a/solution.py
+++ b/solution.py
@@ -88,14 +88,16 @@
     return jnp.where(x < 0.0, q, 1.0 - q), e
 
 
-def forward(take, x, sh, conv, k, kb, gain, nb, w1, b1, w2, b2, ls, h, n, give, before, keep):
+def convolve(take, x, sh, conv, k, kb):
     def bias(r, lanes):
         return jnp.broadcast_to(kb[:, lanes], (W, LANE))
 
     for half in range(2):
         take(half)
         conv_half(x, sh, k, conv, bias, half, False)
-    before()
+
+
+def mix(x, conv, gain, nb, w1, b1, w2, b2, ls, h, n, give, keep):
     for half in range(2):
         rows = slice(half * HR, half * HR + HR)
         c = conv[half * HS : half * HS + HS].reshape(HR, D)
@@ -145,11 +147,12 @@
 
 def train_kernel(
     sources, marked,
-    inputs, cot, k, kb, gain, nb, w1, b1, w2, b2, ls,
-    o_w1, o_w2, o_s1, o_s2, o_k, o_kb, o_gain, o_nb, o_b1, o_b2, o_ls,
+    inputs, cot, probe, k, kb, gain, nb, w1, b1, w2, b2, ls,
+    o_w1, o_w2, o_probe,
     w1f, w2f, w1b, w2b, x, sh, shd, conv, xhat, rstd, nrm, h, gp, mixed, dmb, du, dc, g,
     pt, gkb, ggain, gnb, gb1, gb2, gls, tiles, outgoing, incoming,
     fsend, frecv, bsend, brecv, f_s, f_r, b_s, b_r, w_in, w_out, e_s, e_r, block_of,
+    o_k, o_kb, o_gain, o_nb, o_b1, o_b2, o_ls,
 ):
     s = lax.axis_index("section")
     last = lax.axis_size("section") - 1
@@ -209,8 +212,13 @@
     def fwd_copy(j, half):
         return half_copy(fsend, frecv, (f_s, f_r), j, half, up)
 
-    def bwd_copy(j, half):
-        return half_copy(bsend, brecv, (b_s, b_r), j, half, down)
+    pieces = ((0, HS - 3), (HS - 3, HS), (HS, S))
+
+    def bwd_copy(j, piece):
+        rows = pl.ds(pieces[piece][0], pieces[piece][1] - pieces[piece][0])
+        return to_section(
+            bsend.at[j, rows], brecv.at[j, rows], b_s.at[j, piece], b_r.at[j, piece], down
+        )
 
     def fwd(j):
         rows = pl.ds(pl.multiple_of(j * R, R), R)
@@ -235,12 +243,15 @@
                 fsend[j, half * HS : half * HS + HS] = unpadded(values.reshape(HS, W, D)).astype(BF)
                 fwd_copy(j, half).start()
 
-        forward(
+        convolve(
             lambda half: take(
                 half, s == 0, inputs.at[j], frecv.at[j], fwd_copy(j, half).wait_recv, x.at[j]
             ),
-            x.at[j], sh.at[j], conv, k, kb, gain, nb, w1b, b1, w2b, b2, ls,
-            h.at[rows, :], nrm.at[rows, :], give, before,
+            x.at[j], sh.at[j], conv, k, kb,
+        )
+        before()
+        mix(
+            x.at[j], conv, gain, nb, w1b, b1, w2b, b2, ls, h.at[rows, :], nrm.at[rows, :], give,
             (xhat.at[j], rstd.at[j], gp.at[j], mixed.at[j]),
         )
 
@@ -267,6 +278,11 @@
         loop(D // LANE, per_lanes)
 
     def bwd(j):
+        def send_back(piece):
+            part = slice(*pieces[piece])
+            bsend[j, part] = unpadded(g[part] + conv[part]).astype(BF)
+            bwd_copy(j, piece).start()
+
         def nothing(r, lanes):
             return jnp.zeros((W, LANE), F32)
 
@@ -274,7 +290,12 @@
             base = pl.multiple_of(j * R, R)
             rows = slice(half * HR, half * HR + HR)
             both = half_rows(half, base)
-            take(half, s == last, cot.at[j], brecv.at[j], bwd_copy(j, half).wait_recv, g)
+
+            def arrive(half=half):
+                for piece in ((0, 1), (2,))[half]:
+                    bwd_copy(j, piece).wait_recv()
+
+            take(half, s == last, cot.at[j], brecv.at[j], arrive, g)
             flat = g[half * HS : half * HS + HS].reshape(HR, D)
             dm = flat * ls[...]
             dmb[both, :] = dm.astype(BF)
@@ -299,26 +320,10 @@
             @pl.when(s > 0)
             def _(half=half):
                 conv_half(dc.at[j], shd, k, conv, nothing, half, True)
-
-        @pl.when(s > 0)
-        def _():
-            for half in range(2):
-                part = slice(half * HS, half * HS + HS)
-                bsend[j, part] = unpadded(g[part] + conv[part]).astype(BF)
-                bwd_copy(j, half).start()
-
-        @pl.when((j == 0) & (s < last))
-        def _():
-            kernel_grad(0)
+                for piece in ((0,), (1, 2))[half]:
+                    send_back(piece)
 
     loop(2, bwd)
-
-    stores = []
-
-    def store(src, dst):
-        copy = pltpu.make_async_copy(src, dst, w_out.at[len(stores)])
-        copy.start()
-        stores.append(copy)
 
     for c in range(4):
         cols = pl.ds(c * 512, 512)
@@ -347,9 +352,7 @@
         outgoing[t] = tiles[block_of[t]]
         push_copy(t).start()
 
-    store(w1f, o_w1)
-    store(w2f, o_w2)
-    lax.fori_loop(jnp.where(s == last, 0, 1), 2, lambda j, c: (kernel_grad(j), c)[1], 0)
+    loop(2, kernel_grad)
     for di in range(7):
         for dj in range(7):
             o_k[di, dj] = k[di, dj] - learning_rate * jnp.sum(pt[di, dj], axis=0, keepdims=True)
@@ -359,43 +362,101 @@
     ):
         new[...] = old[...] - learning_rate * grad[...]
 
+    def probe_take(half):
+        take(half, s == 0, probe, frecv.at[2], fwd_copy(2, half).wait_recv, x.at[0])
+
+    def probe_give(half, values):
+        rows = slice(half * HS, half * HS + HS)
+        fsend[2, rows] = unpadded(values.reshape(HS, W, D)).astype(BF)
+
+        @pl.when(s < last)
+        def _():
+            fwd_copy(2, half).start()
+
+        o_probe[rows] = fsend[2, rows, 0:S, :]
+
+    @pl.when(s == 0)
+    def _():
+        convolve(probe_take, x.at[0], shd, conv, o_k, o_kb)
+
     for t in ORDER:
         push_copy(t).wait_recv()
 
-    def chosen(b):
+    def slot_of(b):
         source = sources[b, me]
         z = lax.rem(me // 8 - source // 8 + 4, 4)
         x = lax.rem(lax.rem(me // 2, 4) - lax.rem(source // 2, 4) + 4, 4)
         c = lax.rem(lax.rem(me, 2) + lax.rem(source, 2), 2)
-        return jnp.where(marked[b] == 1, incoming[z * 8 + x * 2 + c], tiles[b])
+        return z * 8 + x * 2 + c
 
     def place_in(b):
-        w1b[:, lanes_of(b)] = chosen(b)
+        w1b[:, lanes_of(b)] = jnp.where(marked[b] == 1, incoming[slot_of(b)], tiles[b])
 
     loop(16, place_in)
-    store(w1b, o_s1)
 
     def place_out(r):
         for c in range(4):
-            w2b[pl.ds(pl.multiple_of(r * D, D), D), pl.ds(c * TILE, TILE)] = chosen(16 + 4 * c + r)
+            b = 16 + 4 * c + r
+            w2b[pl.ds(pl.multiple_of(r * D, D), D), pl.ds(c * TILE, TILE)] = jnp.where(
+                marked[b] == 1, incoming[slot_of(b)], tiles[b]
+            )
 
     loop(4, place_out)
-    store(w2b, o_s2)
+
+    stores = [
+        pltpu.make_async_copy(w1f, o_w1, w_out.at[0]),
+        pltpu.make_async_copy(w2f, o_w2, w_out.at[1]),
+    ]
+
+    def finish():
+        def finish_in(b):
+            lanes = lanes_of(b)
+            w1f[:, lanes] = jnp.where(marked[b] == 1, w1b[:, lanes].astype(F32), w1f[:, lanes])
+
+        def finish_out(r):
+            rows = pl.ds(pl.multiple_of(r * D, D), D)
+            for c in range(4):
+                cols = pl.ds(c * TILE, TILE)
+                w2f[rows, cols] = jnp.where(
+                    marked[16 + 4 * c + r] == 1, w2b[rows, cols].astype(F32), w2f[rows, cols]
+                )
+
+        loop(16, finish_in)
+        stores[0].start()
+        loop(4, finish_out)
+        stores[1].start()
+
+    @pl.when(s > 0)
+    def _():
+        finish()
+        convolve(probe_take, x.at[0], shd, conv, o_k, o_kb)
+
+    mix(
+        x.at[0], conv, o_gain, o_nb, w1b, o_b1, w2b, o_b2, o_ls,
+        h.at[pl.ds(0, R), :], nrm.at[pl.ds(0, R), :], probe_give, None,
+    )
+
+    @pl.when(s == 0)
+    def _():
+        finish()
 
     for copy in stores:
         copy.wait()
     for t in ORDER:
         push_copy(t).wait_send()
-    for j in range(2):
-        for half in range(2):
+    for half in range(2):
+        for j in range(3):
 
             @pl.when(s < last)
             def _(j=j, half=half):
                 fwd_copy(j, half).wait_send()
 
+    for piece in range(3):
+        for j in range(2):
+
             @pl.when(s > 0)
-            def _(j=j, half=half):
-                bwd_copy(j, half).wait_send()
+            def _(j=j, piece=piece):
+                bwd_copy(j, piece).wait_send()
 
 
 def vmem(n):
@@ -412,21 +473,17 @@
     )
 
 
-def train(tables, inputs, cot, small, w1, w2):
+def train(tables, inputs, cot, probe, small, w1, w2):
     k, kb, gain, nb, b1, b2, ls = small
     dma = pltpu.SemaphoreType.DMA
     V = pltpu.VMEM
     shape = jax.ShapeDtypeStruct
-    row = shape((1, D), F32)
     wide = (2, S, W, D)
     return pl.pallas_call(
         train_kernel,
-        out_shape=(
-            shape((D, HID), F32), shape((HID, D), F32), shape((D, HID), BF), shape((HID, D), BF),
-            shape((7, 7, 1, D), F32), row, row, row, shape((1, HID), F32), row, row,
-        ),
-        in_specs=[pl.BlockSpec(memory_space=pltpu.SMEM)] * 2 + vmem(6) + hbm(1) + vmem(1) + hbm(1) + vmem(2),
-        out_specs=hbm(4) + vmem(7),
+        out_shape=(shape((D, HID), F32), shape((HID, D), F32), shape((S, S, D), BF)),
+        in_specs=[pl.BlockSpec(memory_space=pltpu.SMEM)] * 2 + vmem(7) + hbm(1) + vmem(1) + hbm(1) + vmem(2),
+        out_specs=hbm(2) + vmem(1),
         scratch_shapes=[
             V((D, HID), F32), V((HID, D), F32), V((D, HID), BF), V((HID, D), BF),
             V(wide, F32), V((2, 7, S, W, D), F32), V((7, S, W, D), F32), V((S, W, D), F32),
@@ -436,161 +493,15 @@
             V((7, 7, 8, D), F32), V((1, D), F32), V((1, D), F32), V((1, D), F32),
             V((1, HID), F32), V((1, D), F32), V((1, D), F32),
             V((32, D, TILE), BF), V((32, D, TILE), BF), V((32, D, TILE), BF),
-            V(wide, BF), V(wide, BF), V(wide, BF), V(wide, BF),
-            dma((2, 2)), dma((2, 2)), dma((2, 2)), dma((2, 2)), dma((2,)), dma((4,)),
+            V((3, S, W, D), BF), V((3, S, W, D), BF), V(wide, BF), V(wide, BF),
+            dma((3, 2)), dma((3, 2)), dma((2, 3)), dma((2, 3)), dma((2,)), dma((2,)),
             dma((32,)), dma((32,)), pltpu.SMEM((32,), jnp.int32),
+            V((7, 7, 1, D), F32), V((1, D), F32), V((1, D), F32), V((1, D), F32),
+            V((1, HID), F32), V((1, D), F32), V((1, D), F32),
         ],
         compiler_params=params(0, 60),
         name="train",
-    )(*tables, inputs, cot, k, kb, gain, nb, w1, b1, w2, b2, ls)
-
-
-def probe_kernel(
-    probe, k, kb, gain, nb, w1_hbm, b1, w2_hbm, b2, ls, after,
-    out_ref,
-    w1, w2, x, sh, conv, nrm, h, fsend, frecv, f_s, f_r, w_in,
-):
-    s = lax.axis_index("section")
-    last = lax.axis_size("section") - 1
-    up = jnp.minimum(s + 1, last)
-    loads = [
-        pltpu.make_async_copy(w1_hbm, w1, w_in.at[0]),
-        pltpu.make_async_copy(w2_hbm, w2, w_in.at[1]),
-    ]
-    for load in loads:
-        load.start()
-    barrier = pltpu.get_barrier_semaphore()
-    greet_sections(barrier)
-    pl.semaphore_wait(barrier, 2)
-
-    def loaded():
-        for load in loads:
-            load.wait()
-
-    def copy(half):
-        rows = pl.ds(half * HS, HS)
-        return to_section(fsend.at[rows], frecv.at[rows], f_s.at[half], f_r.at[half], up)
-
-    def take(half):
-        rows = slice(half * HS, half * HS + HS)
-
-        @pl.when(s == 0)
-        def _():
-            x[rows, S:W, :] = jnp.zeros((HS, W - S, D), F32)
-            x[rows, 0:S, :] = probe[rows].astype(F32)
-
-        @pl.when(s > 0)
-        def _():
-            copy(half).wait_recv()
-            x[rows] = frecv[rows].astype(F32)
-
-    def give(half, values):
-        rows = slice(half * HS, half * HS + HS)
-        fsend[rows] = unpadded(values.reshape(HS, W, D)).astype(BF)
-
-        @pl.when(s < last)
-        def _():
-            copy(half).start()
-
-        out_ref[rows] = fsend[rows, 0:S, :]
-
-    forward(
-        take, x, sh, conv, k, kb, gain, nb, w1, b1, w2, b2, ls, h, nrm, give, loaded, None
-    )
-
-    @pl.when(s < last)
-    def _():
-        for half in range(2):
-            copy(half).wait_send()
-
-
-def run_probe(probe, small, w1, w2, after):
-    k, kb, gain, nb, b1, b2, ls = small
-    dma = pltpu.SemaphoreType.DMA
-    V = pltpu.VMEM
-    return pl.pallas_call(
-        probe_kernel,
-        out_shape=jax.ShapeDtypeStruct((S, S, D), BF),
-        in_specs=vmem(5) + hbm(1) + vmem(1) + hbm(1) + vmem(2) + hbm(1),
-        out_specs=vmem(1)[0],
-        scratch_shapes=[
-            V((D, HID), BF), V((HID, D), BF), V((S, W, D), F32), V((7, S, W, D), F32), V((S, W, D), F32), V((R, D), BF),
-            V((R, HID), BF), V((S, W, D), BF), V((S, W, D), BF), dma((2,)), dma((2,)), dma((2,)),
-        ],
-        compiler_params=params(1, 24),
-        name="probe",
-    )(probe, k, kb, gain, nb, w1, b1, w2, b2, ls, after)
-
-
-PARTS = 8
-
-
-def finish_kernel(first, *refs):
-    if first:
-        marked, u1, u2, s1, s2, o1, o2, f1, f2, b1, b2, sem, out = refs
-    else:
-        marked, u1, u2, s1, s2, _, _, _, o1, o2, f1, f2, b1, b2, sem, out = refs
-    s = lax.axis_index("section")
-
-    @pl.when(s > 0 if first else s == 0)
-    def _():
-        def rows_of(i):
-            return pl.ds(i * (D // PARTS), D // PARTS), pl.ds(i * (HID // PARTS), HID // PARTS)
-
-        ins, outs = [], []
-        for i in range(PARTS):
-            r1, r2 = rows_of(i)
-            pairs = ((u1, f1, r1), (u2, f2, r2), (s1, b1, r1), (s2, b2, r2))
-            ins.append(
-                [
-                    pltpu.make_async_copy(a.at[r, :], b.at[r, :], sem.at[i, q])
-                    for q, (a, b, r) in enumerate(pairs)
-                ]
-            )
-            outs.append(
-                [
-                    pltpu.make_async_copy(a.at[r, :], b.at[r, :], out.at[i, q])
-                    for q, (a, b, r) in enumerate(((f1, o1, r1), (f2, o2, r2)))
-                ]
-            )
-        for part in ins:
-            for copy in part:
-                copy.start()
-        for i in range(PARTS):
-            r1, r2 = rows_of(i)
-            for copy in ins[i]:
-                copy.wait()
-            for c in range(16):
-                at = (r1, pl.ds(c * TILE, TILE))
-                f1[at] = jnp.where(marked[c] == 1, b1[at].astype(F32), f1[at])
-            outs[i][0].start()
-            for c in range(4):
-                at = (r2, pl.ds(c * TILE, TILE))
-                b = 16 + 4 * c + i // (PARTS // 4)
-                f2[at] = jnp.where(marked[b] == 1, b2[at].astype(F32), f2[at])
-            outs[i][1].start()
-        for part in outs:
-            for copy in part:
-                copy.wait()
-
-
-def finish(marked, weights, earlier):
-    dma = pltpu.SemaphoreType.DMA
-    V = pltpu.VMEM
-    first = not earlier
-    return pl.pallas_call(
-        lambda *refs: finish_kernel(first, *refs),
-        out_shape=(jax.ShapeDtypeStruct((D, HID), F32), jax.ShapeDtypeStruct((HID, D), F32)),
-        in_specs=[pl.BlockSpec(memory_space=pltpu.SMEM)] + hbm(4 + len(earlier)),
-        out_specs=hbm(2),
-        scratch_shapes=[
-            V((D, HID), F32), V((HID, D), F32), V((D, HID), BF), V((HID, D), BF),
-            dma((PARTS, 4)), dma((PARTS, 2)),
-        ],
-        input_output_aliases={} if first else {5: 0, 6: 1},
-        compiler_params=pltpu.CompilerParams(vmem_limit_bytes=24 * 2**20),
-        name="finish" if first else "finish_zero",
-    )(marked, *weights, *earlier)
+    )(*tables, inputs, cot, probe, k, kb, gain, nb, w1, b1, w2, b2, ls)
 
 
 def local(
@@ -602,13 +513,10 @@
         layer_scale[0],
     )
     marked = shuffle_mask[0]
-    res = train(
-        (source_member[0], marked), inputs[0, :, 0], cotangent[0, :, 0], small, w_in[0, 0], w_out[0, 0]
-    )
-    weights, fresh = res[:4], res[4:]
-    earlier = finish(marked, weights, ())
-    out = run_probe(probe[0, 0], fresh, weights[2], weights[3], earlier[0])
-    new_in, new_out = finish(marked, weights, (*earlier, out))
+    new_in, new_out, out = train(
+        (source_member[0], marked), inputs[0, :, 0], cotangent[0, :, 0], probe[0, 0], small,
+        w_in[0, 0], w_out[0, 0],
+    )
     return new_in[None, None], new_out[None, None], out[None, None, None]
 
 

time: 179 us -> 168 us (0.939)
  Pallas kernels: 164 us -> 158 us
  local copies, waits for them, and re-layouts: 12.7 us -> 9.79 us
    pallas_call x3 -> x0, Pallas kernels: 55.4 us -> none  [the longest x1 49.1 us: run_probe(): pl.pallas_call(probe_kernel, out_shape=jax.ShapeDtypeStruct((S, S, D), BF...]
    pallas_call x1, Pallas kernels: 109 us -> 158 us  [train(): pl.pallas_call(train_kernel, out_shape=(shape((D, HID), F32), shape((HID,...]
    unnamed x35 -> x7, local copies, waits for them, and re-layouts: 10.5 us -> 7.56 us
where the time goes in v3:
time: 168 us
  Pallas kernels  158 us (94%)
  local copies, waits for them, and re-layouts  9.79 us (6%)
    pallas_call x1, Pallas kernels, train(): pl.pallas_call(train_kernel, out_shape=(shape((D, HID), F32), shape((HID,...  158 us
    unnamed x7, local copies, waits for them, and re-layouts  7.56 us

profile of v3, /device:TPU:56, one launch (start us, length us, event | category | flops | bytes accessed | tf_op | source)
XLA Modules:
  0.0 167.9 jit_solution(3179602854773386811)
XLA Ops:
  0.6 2.2 %copy_bitcast_fusion = (bf16[2,14,14,512]{3,2,1,0:T(8,128)(2,1)}, bf16[2,14,14,512]{3,2,1,0:T(8,128)(2,1)}) fusion(bf16[1,2,1,14,14,512]{5,1,4,3,2,0:T(2,128)(2,1)} %param.15, bf16[1,2,1,14,14,512]{5,1,4,3,2,0:T(2,128)(2,1)} %param.14), kind=kLoop, calls=%fused_computation | loop fusion | bytes 1605632 | tf_op jit(solution)/shard_map/squeeze | solution.py:517
  2.9 157.5 %train.1 = (f32[512,2048]{1,0:T(8,128)}, f32[2048,512]{1,0:T(8,128)}, bf16[14,14,512]{2,1,0:T(8,128)(2,1)}) custom-call(s32[32,32]{1,0:T(8,128)} %bitcast.26, s32[32]{0:T(128)} %bitcast.33, bf16[2,14,14,512]{3,2,1,0:T(8,128)(2,1)} %get-tuple-element.10.inputs, bf16[2,14,14,512]{3,2,1,0:T(8,128)(2,1)} %get-tuple-element.9.cot, bf16[14,14,512]{2,1,0:T(8,128)(2,1)} %bitcast.24, ...), custom_call_target="tpu_custom_call" | custom-call | tf_op jit(solution)/shard_map/train/pallas_call | solution.py:482
  160.4 0.0 copy-start
  160.4 4.8 %copy.24 = f32[1,1,512,2048]{3,2,1,0:T(8,128)} copy(f32[1,1,512,2048]{3,2,1,0:T(8,128)} %bitcast.22) | data formatting | bytes 8388608
  165.2 0.0 copy-done
  165.2 0.0 copy-start.1
  165.2 2.0 %copy.25 = f32[1,1,2048,512]{3,2,1,0:T(8,128)} copy(f32[1,1,2048,512]{3,2,1,0:T(8,128)S(1)} %bitcast.21) | data formatting | bytes 8388608
  167.3 0.0 copy-done.1
  167.3 0.7 copy.26
Async XLA Ops:
  160.4 4.9 %copy-start = (f32[2048,512]{1,0:T(8,128)S(1)}, f32[2048,512]{1,0:T(8,128)}, u32[]{:S(2)}) copy-start(f32[2048,512]{1,0:T(8,128)} %get-tuple-element.7) | copy-start | bytes 12582916
  165.2 2.0 %copy-start.1 = (bf16[14,14,512]{2,1,0:T(8,128)(2,1)S(1)}, bf16[14,14,512]{2,1,0:T(8,128)(2,1)}, u32[]{:S(2)}) copy-start(bf16[14,14,512]{2,1,0:T(8,128)(2,1)} %get-tuple-element.8) | copy-start | bytes 602116

commit v4 on v3

--- a/solution.py
+++ b/solution.py
@@ -25,6 +25,13 @@
     (0, 2), (2, 0), (2, 2), (1, 2), (2, 1), (3, 2), (2, 3),
 )
 ORDER = tuple(z * 8 + x * 2 + c for c in (1, 0) for z, x in CHIPS if (z, x, c) != (0, 0, 0))
+
+RELAYED = tuple(z * 8 + x * 2 + c for z, x, c in ((2, 2, 0), (2, 2, 1), (1, 2, 1), (2, 1, 1)))
+EARLY = 14
+DIRECT = tuple(t for t in ORDER if t not in RELAYED)
+SEQUENCE = tuple(
+    t for i, r in enumerate(RELAYED) for t in (DIRECT[2 * i], r, DIRECT[2 * i + 1])
+) + DIRECT[2 * len(RELAYED) :]
 
 
 def at_distance(me, t, sign=1):
@@ -151,7 +158,7 @@
     o_w1, o_w2, o_probe,
     w1f, w2f, w1b, w2b, x, sh, shd, conv, xhat, rstd, nrm, h, gp, mixed, dmb, du, dc, g,
     pt, gkb, ggain, gnb, gb1, gb2, gls, tiles, outgoing, incoming,
-    fsend, frecv, bsend, brecv, f_s, f_r, b_s, b_r, w_in, w_out, e_s, e_r, block_of,
+    fsend, frecv, bsend, brecv, f_s, f_r, b_s, b_r, w_in, w_out, e_s, e_r, block_of, relay, r_s, r_r,
     o_k, o_kb, o_gain, o_nb, o_b1, o_b2, o_ls,
 ):
     s = lax.axis_index("section")
@@ -348,9 +355,64 @@
             device_id_type=MESH,
         )
 
-    for t in ORDER:
+    partner = last - s
+
+    def relay_copy(i):
+        return to_section(
+            outgoing.at[RELAYED[i]], relay.at[0, i], e_s.at[RELAYED[i]], r_r.at[0, i], partner
+        )
+
+    def relay_across(i):
+        return pltpu.make_async_remote_copy(
+            src_ref=relay.at[0, i],
+            dst_ref=relay.at[1, i],
+            send_sem=r_s.at[0, i],
+            recv_sem=r_r.at[1, i],
+            device_id={"member": at_distance(me, RELAYED[i])},
+            device_id_type=MESH,
+        )
+
+    def relay_back(i):
+        return to_section(
+            relay.at[1, i], incoming.at[RELAYED[i]], r_s.at[1, i], e_r.at[RELAYED[i]], partner
+        )
+
+    def push(t):
         outgoing[t] = tiles[block_of[t]]
-        push_copy(t).start()
+        if t in RELAYED:
+
+            @pl.when(s == 0)
+            def _():
+                relay_copy(RELAYED.index(t)).start()
+
+            @pl.when(s > 0)
+            def _():
+                push_copy(t).start()
+        else:
+            push_copy(t).start()
+
+    for t in SEQUENCE[:EARLY]:
+        push(t)
+
+    later = list(SEQUENCE[EARLY:])
+    for i in range(len(RELAYED) + 1):
+        if i < len(RELAYED):
+
+            @pl.when(s == last)
+            def _(i=i):
+                relay_copy(i).wait_recv()
+                relay_across(i).start()
+
+        if i > 0:
+
+            @pl.when(s == last)
+            def _(i=i - 1):
+                relay_across(i).wait_recv()
+                relay_back(i).start()
+
+        push(later.pop(0))
+    for t in later:
+        push(t)
 
     loop(2, kernel_grad)
     for di in range(7):
@@ -444,6 +506,13 @@
         copy.wait()
     for t in ORDER:
         push_copy(t).wait_send()
+
+    @pl.when(s == last)
+    def _():
+        for i in range(len(RELAYED)):
+            relay_across(i).wait_send()
+            relay_back(i).wait_send()
+
     for half in range(2):
         for j in range(3):
 
@@ -496,6 +565,7 @@
             V((3, S, W, D), BF), V((3, S, W, D), BF), V(wide, BF), V(wide, BF),
             dma((3, 2)), dma((3, 2)), dma((2, 3)), dma((2, 3)), dma((2,)), dma((2,)),
             dma((32,)), dma((32,)), pltpu.SMEM((32,), jnp.int32),
+            V((2, len(RELAYED), D, TILE), BF), dma((2, len(RELAYED))), dma((2, len(RELAYED))),
             V((7, 7, 1, D), F32), V((1, D), F32), V((1, D), F32), V((1, D), F32),
             V((1, HID), F32), V((1, D), F32), V((1, D), F32),
         ],

time: 168 us -> 159 us (0.946); the launches traced: 168 us -> 157 us
  Pallas kernels: 158 us -> 146 us
    pallas_call x1, Pallas kernels: 158 us -> 146 us  [train(): pl.pallas_call(train_kernel, out_shape=(shape((D, HID), F32), shape((HID,...]
where the time goes in v4:
time: 159 us; the launch traced here: 157 us
  Pallas kernels  146 us (92%)
  local copies, waits for them, and re-layouts  9.79 us (6%)
    pallas_call x1, Pallas kernels, train(): pl.pallas_call(train_kernel, out_shape=(shape((D, HID), F32), shape((HID,...  146 us
    unnamed x7, local copies, waits for them, and re-layouts  7.56 us

profile of v4, /device:TPU:56, one launch (start us, length us, event | category | flops | bytes accessed | tf_op | source)
XLA Modules:
  0.0 156.9 jit_solution(15481143105518674328)
XLA Ops:
  0.6 2.2 %copy_bitcast_fusion = (bf16[2,14,14,512]{3,2,1,0:T(8,128)(2,1)}, bf16[2,14,14,512]{3,2,1,0:T(8,128)(2,1)}) fusion(bf16[1,2,1,14,14,512]{5,1,4,3,2,0:T(2,128)(2,1)} %param.15, bf16[1,2,1,14,14,512]{5,1,4,3,2,0:T(2,128)(2,1)} %param.14), kind=kLoop, calls=%fused_computation | loop fusion | bytes 1605632 | tf_op jit(solution)/shard_map/squeeze | solution.py:587
  2.9 146.5 %train.1 = (f32[512,2048]{1,0:T(8,128)}, f32[2048,512]{1,0:T(8,128)}, bf16[14,14,512]{2,1,0:T(8,128)(2,1)}) custom-call(s32[32,32]{1,0:T(8,128)} %bitcast.26, s32[32]{0:T(128)} %bitcast.33, bf16[2,14,14,512]{3,2,1,0:T(8,128)(2,1)} %get-tuple-element.10.inputs, bf16[2,14,14,512]{3,2,1,0:T(8,128)(2,1)} %get-tuple-element.9.cot, bf16[14,14,512]{2,1,0:T(8,128)(2,1)} %bitcast.24, ...), custom_call_target="tpu_custom_call" | custom-call | tf_op jit(solution)/shard_map/train/pallas_call | solution.py:551
  149.3 0.0 copy-start
  149.3 4.8 %copy.24 = f32[1,1,512,2048]{3,2,1,0:T(8,128)} copy(f32[1,1,512,2048]{3,2,1,0:T(8,128)} %bitcast.22) | data formatting | bytes 8388608
  154.2 0.0 copy-done
  154.2 0.0 copy-start.1
  154.2 2.0 %copy.25 = f32[1,1,2048,512]{3,2,1,0:T(8,128)} copy(f32[1,1,2048,512]{3,2,1,0:T(8,128)S(1)} %bitcast.21) | data formatting | bytes 8388608
  156.2 0.0 copy-done.1
  156.2 0.7 copy.26
Async XLA Ops:
  149.3 4.9 %copy-start = (f32[2048,512]{1,0:T(8,128)S(1)}, f32[2048,512]{1,0:T(8,128)}, u32[]{:S(2)}) copy-start(f32[2048,512]{1,0:T(8,128)} %get-tuple-element.7) | copy-start | bytes 12582916
  154.2 2.0 %copy-start.1 = (bf16[14,14,512]{2,1,0:T(8,128)(2,1)S(1)}, bf16[14,14,512]{2,1,0:T(8,128)(2,1)}, u32[]{:S(2)}) copy-start(bf16[14,14,512]{2,1,0:T(8,128)(2,1)} %get-tuple-element.8) | copy-start | bytes 602116

commit v5 on v4

--- a/solution.py
+++ b/solution.py
@@ -26,8 +26,11 @@
 )
 ORDER = tuple(z * 8 + x * 2 + c for c in (1, 0) for z, x in CHIPS if (z, x, c) != (0, 0, 0))
 
-RELAYED = tuple(z * 8 + x * 2 + c for z, x, c in ((2, 2, 0), (2, 2, 1), (1, 2, 1), (2, 1, 1)))
+RELAYED = tuple(
+    z * 8 + x * 2 + c for z, x, c in ((2, 2, 0), (2, 2, 1), (1, 2, 1), (2, 1, 1), (3, 2, 1))
+)
 EARLY = 14
+BOTH = 0
 DIRECT = tuple(t for t in ORDER if t not in RELAYED)
 SEQUENCE = tuple(
     t for i, r in enumerate(RELAYED) for t in (DIRECT[2 * i], r, DIRECT[2 * i + 1])
@@ -181,7 +184,6 @@
         )
     for ref in (pt, gkb, ggain, gnb, gb1, gb2, gls):
         ref[...] = jnp.zeros_like(ref)
-    pl.semaphore_wait(barrier, 2 + len(ORDER))
 
     def tables():
         def per_slot(t):
@@ -233,6 +235,7 @@
         def before():
             @pl.when(j == 0)
             def _():
+                pl.semaphore_wait(barrier, 2 + len(ORDER))
                 for load in loads:
                     load.wait()
 
@@ -357,6 +360,12 @@
 
     partner = last - s
 
+    def is_relayed(i):
+        return s < (2 if i < BOTH else 1)
+
+    def is_relay(i):
+        return partner < (2 if i < BOTH else 1)
+
     def relay_copy(i):
         return to_section(
             outgoing.at[RELAYED[i]], relay.at[0, i], e_s.at[RELAYED[i]], r_r.at[0, i], partner
@@ -381,11 +390,13 @@
         outgoing[t] = tiles[block_of[t]]
         if t in RELAYED:
 
-            @pl.when(s == 0)
+            i = RELAYED.index(t)
+
+            @pl.when(is_relayed(i))
             def _():
-                relay_copy(RELAYED.index(t)).start()
-
-            @pl.when(s > 0)
+                relay_copy(i).start()
+
+            @pl.when(jnp.logical_not(is_relayed(i)))
             def _():
                 push_copy(t).start()
         else:
@@ -398,14 +409,14 @@
     for i in range(len(RELAYED) + 1):
         if i < len(RELAYED):
 
-            @pl.when(s == last)
+            @pl.when(is_relay(i))
             def _(i=i):
                 relay_copy(i).wait_recv()
                 relay_across(i).start()
 
         if i > 0:
 
-            @pl.when(s == last)
+            @pl.when(is_relay(i - 1))
             def _(i=i - 1):
                 relay_across(i).wait_recv()
                 relay_back(i).start()
@@ -507,9 +518,10 @@
     for t in ORDER:
         push_copy(t).wait_send()
 
-    @pl.when(s == last)
-    def _():
-        for i in range(len(RELAYED)):
+    for i in range(len(RELAYED)):
+
+        @pl.when(is_relay(i))
+        def _(i=i):
             relay_across(i).wait_send()
             relay_back(i).wait_send()
 

time: 159 us -> 157 us (0.987)
  no operation moved by 1% of the time
where the time goes in v5:
time: 157 us; the launch traced here: 156 us
  Pallas kernels  145 us (92%)
  local copies, waits for them, and re-layouts  9.79 us (6%)
    pallas_call x1, Pallas kernels, train(): pl.pallas_call(train_kernel, out_shape=(shape((D, HID), F32), shape((HID,...  145 us
    unnamed x7, local copies, waits for them, and re-layouts  7.56 us

profile of v5, /device:TPU:56, one launch (start us, length us, event | category | flops | bytes accessed | tf_op | source)
XLA Modules:
  0.0 155.8 jit_solution(18392327474414388912)
XLA Ops:
  0.6 2.2 %copy_bitcast_fusion = (bf16[2,14,14,512]{3,2,1,0:T(8,128)(2,1)}, bf16[2,14,14,512]{3,2,1,0:T(8,128)(2,1)}) fusion(bf16[1,2,1,14,14,512]{5,1,4,3,2,0:T(2,128)(2,1)} %param.15, bf16[1,2,1,14,14,512]{5,1,4,3,2,0:T(2,128)(2,1)} %param.14), kind=kLoop, calls=%fused_computation | loop fusion | bytes 1605632 | tf_op jit(solution)/shard_map/squeeze | solution.py:599
  2.9 145.4 %train.1 = (f32[512,2048]{1,0:T(8,128)}, f32[2048,512]{1,0:T(8,128)}, bf16[14,14,512]{2,1,0:T(8,128)(2,1)}) custom-call(s32[32,32]{1,0:T(8,128)} %bitcast.26, s32[32]{0:T(128)} %bitcast.33, bf16[2,14,14,512]{3,2,1,0:T(8,128)(2,1)} %get-tuple-element.10.inputs, bf16[2,14,14,512]{3,2,1,0:T(8,128)(2,1)} %get-tuple-element.9.cot, bf16[14,14,512]{2,1,0:T(8,128)(2,1)} %bitcast.24, ...), custom_call_target="tpu_custom_call" | custom-call | tf_op jit(solution)/shard_map/train/pallas_call | solution.py:563
  148.3 0.0 copy-start
  148.3 4.8 %copy.24 = f32[1,1,512,2048]{3,2,1,0:T(8,128)} copy(f32[1,1,512,2048]{3,2,1,0:T(8,128)} %bitcast.22) | data formatting | bytes 8388608
  153.1 0.0 copy-done
  153.1 0.0 copy-start.1
  153.1 2.0 %copy.25 = f32[1,1,2048,512]{3,2,1,0:T(8,128)} copy(f32[1,1,2048,512]{3,2,1,0:T(8,128)S(1)} %bitcast.21) | data formatting | bytes 8388608
  155.1 0.0 copy-done.1
  155.2 0.7 copy.26
Async XLA Ops:
  148.3 4.9 %copy-start = (f32[2048,512]{1,0:T(8,128)S(1)}, f32[2048,512]{1,0:T(8,128)}, u32[]{:S(2)}) copy-start(f32[2048,512]{1,0:T(8,128)} %get-tuple-element.7) | copy-start | bytes 12582916
  153.1 2.0 %copy-start.1 = (bf16[14,14,512]{2,1,0:T(8,128)(2,1)S(1)}, bf16[14,14,512]{2,1,0:T(8,128)(2,1)}, u32[]{:S(2)}) copy-start(bf16[14,14,512]{2,1,0:T(8,128)(2,1)} %get-tuple-element.8) | copy-start | bytes 602116
